TPU v7x, 32 devices: a whole 2x2x4 slice. The times are simulated.
32 devices in a mesh: half: 2 (over x), gx: 4 (over z), gy: 4 (over y, core).
Axes of the slice: x: 2, y: 2, z: 4, core: 2. Of those that a mesh axis runs over, the one named last changes fastest.
Arguments:
- state: float32 [2, 20, 8, 64, 128], P('half', None, 'gx', 'gy'), may hold values from -4 to 4
- levels: int32 [4, 8, 64], P(None, 'gx', 'gy'), may hold values from 0 to 128
- old_flux: float32 [2, 8, 64, 128], P(None, 'gx', 'gy'), may hold values from -4 to 4
- eco_prey: int32 [19], replicated, may hold values from 0 to 18
- eco_rate: float32 [19], replicated, may hold values from 0.3 to 3
Outputs:
- state_next: float32 [2, 20, 8, 64, 128], P('half', None, 'gx', 'gy')
All inputs are finite; a program needn't handle non-finite values.
Results may differ from a plain program's by a relative error of at most 0.00013.
Values sent between devices are 32-bit elements; how exact they have to be, the bound alone decides.
A program may use at most 64 MiB of HBM per device.

v0:
```python
import jax
import jax.numpy as jnp
from jax import lax
from jax.sharding import PartitionSpec as P

NSUB = 4


DT = 0.1
NU = 1.0
CORIOLIS = 0.5
DRAG = 0.1
MORTALITY = 0.1
HEATING = 2.0
SURFACE = 8.0


def extended_2(shard, sides, width):
    for axis, dim in sides:
        peers, length = (lax.axis_size(axis), shard.shape[dim])
        up = [(i, (i + 1) % peers) for i in range(peers - 1)]
        down = [(j, i) for i, j in up]
        last = lax.slice_in_dim(shard, length - width, length, axis=dim)
        leading = lax.slice_in_dim(shard, 0, width, axis=dim)
        before = lax.ppermute(last, axis, up)
        after = lax.ppermute(leading, axis, down)
        shard = jnp.concatenate([before, shard, after], axis=dim)
    return shard


def from_behind(shard, axis, by):
    peers = lax.axis_size(axis)
    pairs = [(i, i + by) for i in range(peers) if 0 <= i + by < peers]
    return lax.ppermute(shard, axis, pairs)


def to_fine(coarse):
    fields = coarse.shape[0] // 4
    size_x, size_y, depth = (coarse.shape[1], coarse.shape[2], coarse.shape[3])
    split = coarse.reshape(fields, 2, 2, size_x, size_y, depth).transpose(0, 3, 1, 4, 2, 5)
    return split.reshape(fields, 2 * size_x, 2 * size_y, depth)


def to_coarse(fine_cells):
    fields, fine_x, fine_y, depth = fine_cells.shape
    split = fine_cells.reshape(fields, fine_x // 2, 2, fine_y // 2, 2, depth).transpose(
        0, 2, 4, 1, 3, 5
    )
    return split.reshape(fields * 4, fine_x // 2, fine_y // 2, depth)


def fine_levels(levels):
    size_x, size_y = (levels.shape[1], levels.shape[2])
    return (
        levels.reshape(2, 2, size_x, size_y).transpose(2, 0, 3, 1).reshape(2 * size_x, 2 * size_y)
    )


def wet_of(levels, depth):
    shape = levels.shape + (depth,)
    return (lax.broadcasted_iota(jnp.int32, shape, len(shape) - 1) < levels[..., None]).astype(
        jnp.float32
    )


def trim_margin(values, margin, keep):
    cut = margin - keep
    if cut == 0:
        return values
    return values[..., cut : values.shape[-3] - cut, cut : values.shape[-2] - cut, :]


def ocean_substep(fields, wet_mask, heating):
    centre = fields[:, 1:-1, 1:-1]
    to_east = fields[:, 2:, 1:-1]
    to_west = fields[:, :-2, 1:-1]
    to_north = fields[:, 1:-1, 2:]
    to_south = fields[:, 1:-1, :-2]
    speed_east = centre[0]
    speed_north = centre[1]
    advect = speed_east * (to_east - to_west) * 0.5 + speed_north * (to_north - to_south) * 0.5
    spread = to_east + to_west + to_north + to_south - 4.0 * centre
    zeroes = jnp.zeros_like(speed_east)
    forcing = jnp.stack(
        [
            CORIOLIS * speed_north - DRAG * speed_east,
            -CORIOLIS * speed_east - DRAG * speed_north,
            zeroes + heating,
            zeroes,
            zeroes + 1.0,
        ]
    )
    return wet_mask * (centre + DT * (NU * spread - advect + forcing))


def tracer_substep(fields, wet_mask, volume_flux, onehot, eco_rate):
    species = eco_rate.shape[0]
    centre = fields[:, 1:-1, 1:-1]
    to_east = fields[:, 2:, 1:-1]
    to_west = fields[:, :-2, 1:-1]
    to_north = fields[:, 1:-1, 2:]
    to_south = fields[:, 1:-1, :-2]
    advect = (
        volume_flux[0] * (to_east - to_west) * 0.5 + volume_flux[1] * (to_north - to_south) * 0.5
    )
    spread = to_east + to_west + to_north + to_south - 4.0 * centre
    living = centre[:species]
    prey_values = jnp.einsum("ts,sxyk->txyk", onehot, living, precision=lax.Precision.HIGHEST)
    growth = eco_rate[:, None, None, None] * living * jnp.tanh(prey_values) - MORTALITY * living
    reaction = jnp.concatenate([growth, jnp.zeros_like(centre[species:])], axis=0)
    return wet_mask * (centre + DT * (NU * spread - advect + reaction))


def coarse_mean(fine_cells):
    coarse = to_coarse(fine_cells)
    return (
        coarse.reshape(
            fine_cells.shape[0], 4, coarse.shape[1], coarse.shape[2], coarse.shape[3]
        ).sum(axis=1)
        * 0.25
    )


def absorption(tracer, wet_mask, above_table):
    attenuation = wet_mask * (0.03 + 0.05 * jax.nn.softplus(tracer[0]))
    overhead = jnp.einsum("xyk,kl->xyl", attenuation, above_table, precision=lax.Precision.HIGHEST)
    return SURFACE * jnp.exp(-overhead) * (1.0 - jnp.exp(-attenuation))


def advance(
    is_ocean,
    extended,
    wide,
    steps,
    wet_fine,
    fine_margin,
    wet_coarse,
    coarse_margin,
    volume_flux,
    flux_margin,
    heating,
    running,
    onehot,
    eco_rate,
):

    def ocean_part():
        fine_cells = trim_margin(to_fine(extended), 2 * wide, steps)
        summed = running
        remain = steps - 1
        fine_cells = ocean_substep(fine_cells, trim_margin(wet_fine, fine_margin, remain), heating)
        summed = summed + coarse_mean(trim_margin(fine_cells[0:2], remain, 0))
        return (to_coarse(fine_cells), summed)

    def tracer_part():
        tracer = trim_margin(extended, wide, steps)
        remain = steps - 1
        tracer = tracer_substep(
            tracer,
            trim_margin(wet_coarse, coarse_margin, remain),
            trim_margin(volume_flux, flux_margin, remain),
            onehot,
            eco_rate,
        )
        return (tracer, running)

    return lax.cond(is_ocean, ocean_part, tracer_part)


def rim_single(own_block):
    return extended_2(own_block, (("gx", 1), ("gy", 2)), 1)


def body(state, levels, old_flux, eco_prey, eco_rate):
    depth = state.shape[-1]
    size_x, size_y = (state.shape[2], state.shape[3])
    species = eco_rate.shape[0]
    is_ocean = lax.axis_index("half") == 0
    onehot = (eco_prey[:, None] == lax.broadcasted_iota(jnp.int32, (species, species), 1)).astype(
        jnp.float32
    )
    above_table = (
        lax.broadcasted_iota(jnp.int32, (depth, depth), 0)
        < lax.broadcasted_iota(jnp.int32, (depth, depth), 1)
    ).astype(jnp.float32)
    wet_channels = wet_of(levels, depth)
    wet_fine = wet_of(fine_levels(levels), depth)
    wet_coarse = wet_of(jnp.max(levels, axis=0), depth)
    own_block = state[0]
    channels = own_block.shape[0]
    own_block = lax.cond(
        is_ocean,
        lambda: (
            own_block.reshape(channels // 4, 4, size_x, size_y, depth) * wet_channels[None]
        ).reshape(channels, size_x, size_y, depth),
        lambda: own_block * wet_coarse,
    )
    running = jnp.zeros((2, size_x, size_y, depth), jnp.float32)
    for substep in range(NSUB):
        extended = rim_single(own_block)
        own_block, running = advance(
            is_ocean,
            extended,
            1,
            1,
            wet_fine,
            0,
            wet_coarse,
            0,
            old_flux,
            0,
            0.0,
            running,
            onehot,
            eco_rate,
        )
    new_flux = running / NSUB
    absorbed = lax.cond(
        is_ocean,
        lambda: jnp.zeros((size_x, size_y, depth), jnp.float32),
        lambda: absorption(own_block, wet_coarse, above_table),
    )
    flux_arrived = from_behind(new_flux, "half", 1)
    light_arrived = from_behind(absorbed[None], "half", -1)
    heating = HEATING * to_fine(jnp.broadcast_to(light_arrived, (4, size_x, size_y, depth)))[0]
    extended = rim_single(own_block)
    own_block, running = advance(
        is_ocean,
        extended,
        1,
        1,
        wet_fine,
        0,
        wet_coarse,
        0,
        flux_arrived,
        0,
        heating,
        running,
        onehot,
        eco_rate,
    )
    return own_block[None]


def solution(mesh):
    placed = (
        P("half", None, "gx", "gy", None),
        P(None, "gx", "gy"),
        P(None, "gx", "gy", None),
        P(),
        P(),
    )
    return jax.shard_map(
        body,
        mesh=mesh,
        in_specs=placed,
        out_specs=P("half", None, "gx", "gy", None),
        check_vma=False,
    )
```

profile of v0, /device:TPU:3, one launch (start us, length us, event | category | flops | bytes accessed | tf_op | source)
XLA Modules:
  0.0 104.8 jit_solution(12622516713282124748)
XLA Ops:
  2.0 3.2 %collective-permute-start = (f32[20,1,16,128]{3,2,1,0:T(8,128)S(1)}, f32[20,1,16,128]{3,2,1,0:T(8,128)S(1)}, u32[]{:S(2)}, u32[]{:S(2)}) collective-permute-start(f32[20,1,16,128]{3,2,1,0:T(8,128)S(1)} %get-tuple-element.463), channel_id=1, source_target_pairs={{0,4},{4,8},{8,12},{1,5},{5,9},{9,13},{2,6},{6,10},{10,14},{3,7},{... | collective-permute-start | bytes 491528 | tf_op jit(solution)/shard_map/ppermute | solution.py:25
  5.3 1.3 %collective-permute-start.1 = (f32[20,1,16,128]{3,2,1,0:T(8,128)S(1)}, f32[20,1,16,128]{3,2,1,0:T(8,128)S(1)}, u32[]{:S(2)}, u32[]{:S(2)}) collective-permute-start(f32[20,1,16,128]{3,2,1,0:T(8,128)S(1)} %get-tuple-element.464), channel_id=1, source_target_pairs={{4,0},{8,4},{12,8},{5,1},{9,5},{13,9},{6,2},{10,6},{14,10},{7,3},{... | collective-permute-start | bytes 491528 | tf_op jit(solution)/shard_map/ppermute | solution.py:26
  8.1 3.8 %collective-permute-done.1 = f32[20,1,16,128]{3,2,1,0:T(8,128)S(1)} collective-permute-done((f32[20,1,16,128]{3,2,1,0:T(8,128)S(1)}, f32[20,1,16,128]{3,2,1,0:T(8,128)S(1)}, u32[]{:S(2)}, u32[]{:S(2)}) %collective-permute-start.1) | collective-permute-done | bytes 163872 | tf_op jit(solution)/shard_map/ppermute | solution.py:26
  12.0 4.9 %collective-permute-start.2 = (f32[20,4,1,128]{3,2,1,0:T(1,128)S(1)}, f32[20,4,1,128]{3,2,1,0:T(1,128)S(1)}, u32[]{:S(2)}, u32[]{:S(2)}) collective-permute-start(f32[20,4,1,128]{3,2,1,0:T(1,128)S(1)} %get-tuple-element.453), channel_id=1, source_target_pairs={{0,1},{1,2},{2,3},{4,5},{5,6},{6,7},{8,9},{9,10},{10,11},{12,13},{... | collective-permute-start | bytes 122888 | tf_op jit(solution)/shard_map/ppermute | solution.py:25
  17.0 1.9 %collective-permute-start.3 = (f32[20,4,1,128]{3,2,1,0:T(1,128)S(1)}, f32[20,4,1,128]{3,2,1,0:T(1,128)S(1)}, u32[]{:S(2)}, u32[]{:S(2)}) collective-permute-start(f32[20,4,1,128]{3,2,1,0:T(1,128)S(1)} %get-tuple-element.454), channel_id=1, source_target_pairs={{1,0},{2,1},{3,2},{5,4},{6,5},{7,6},{9,8},{10,9},{11,10},{13,12},{... | collective-permute-start | bytes 122888 | tf_op jit(solution)/shard_map/ppermute | solution.py:26
  19.0 3.3 %collective-permute-done.3 = f32[20,4,1,128]{3,2,1,0:T(1,128)S(1)} collective-permute-done((f32[20,4,1,128]{3,2,1,0:T(1,128)S(1)}, f32[20,4,1,128]{3,2,1,0:T(1,128)S(1)}, u32[]{:S(2)}, u32[]{:S(2)}) %collective-permute-start.3) | collective-permute-done | bytes 40992 | tf_op jit(solution)/shard_map/ppermute | solution.py:26
  23.1 2.0 %conditional.8 = (f32[20,2,16,128]{3,2,1,0:T(8,128)S(1)}, f32[2,2,16,128]{3,1,2,0:T(2,128)S(1)}) conditional(s32[]{:T(128)} %convert_element_type.24, (f32[2,16,128]{2,1,0:T(8,128)S(1)}, f32[20,4,16,128]{3,2,1,0:T(8,128)S(1)}, f32[20,4,18,128]{3,2,1,0:T(8,128)S(1)}, f32[20,2,16,128]{3,2,1,0:T(8,128)S(1)}, f32[2,2,16,128]{3,2,1,0:T(8,128)S(1)}, ...), branch_computations={%region_3.0_spmd, %region_4.0_spmd} | conditional | flops 19365888 | bytes 7631380 | solution.py:167
  25.1 3.2 %collective-permute-start.4 = (f32[20,1,16,128]{3,2,1,0:T(8,128)S(1)}, f32[20,1,16,128]{3,2,1,0:T(8,128)S(1)}, u32[]{:S(2)}, u32[]{:S(2)}) collective-permute-start(f32[20,1,16,128]{3,2,1,0:T(8,128)S(1)} %get-tuple-element.462), channel_id=1, source_target_pairs={{0,4},{4,8},{8,12},{1,5},{5,9},{9,13},{2,6},{6,10},{10,14},{3,7},{... | collective-permute-start | bytes 491528 | tf_op jit(solution)/shard_map/ppermute | solution.py:25
  30.6 4.1 %collective-permute-done.5 = f32[20,1,16,128]{3,2,1,0:T(8,128)S(1)} collective-permute-done((f32[20,1,16,128]{3,2,1,0:T(8,128)S(1)}, f32[20,1,16,128]{3,2,1,0:T(8,128)S(1)}, u32[]{:S(2)}, u32[]{:S(2)}) %collective-permute-start.5) | collective-permute-done | bytes 163872 | tf_op jit(solution)/shard_map/ppermute | solution.py:26
  34.8 3.0 %collective-permute-start.6 = (f32[20,4,1,128]{3,2,1,0:T(1,128)S(1)}, f32[20,4,1,128]{3,2,1,0:T(1,128)S(1)}, u32[]{:S(2)}, u32[]{:S(2)}) collective-permute-start(f32[20,4,1,128]{3,2,1,0:T(1,128)S(1)} %get-tuple-element.451), channel_id=1, source_target_pairs={{0,1},{1,2},{2,3},{4,5},{5,6},{6,7},{8,9},{9,10},{10,11},{12,13},{... | collective-permute-start | bytes 122888 | tf_op jit(solution)/shard_map/ppermute | solution.py:25
  37.8 1.9 %collective-permute-start.7 = (f32[20,4,1,128]{3,2,1,0:T(1,128)S(1)}, f32[20,4,1,128]{3,2,1,0:T(1,128)S(1)}, u32[]{:S(2)}, u32[]{:S(2)}) collective-permute-start(f32[20,4,1,128]{3,2,1,0:T(1,128)S(1)} %get-tuple-element.452), channel_id=1, source_target_pairs={{1,0},{2,1},{3,2},{5,4},{6,5},{7,6},{9,8},{10,9},{11,10},{13,12},{... | collective-permute-start | bytes 122888 | tf_op jit(solution)/shard_map/ppermute | solution.py:26
  39.8 3.4 %collective-permute-done.7 = f32[20,4,1,128]{3,2,1,0:T(1,128)S(1)} collective-permute-done((f32[20,4,1,128]{3,2,1,0:T(1,128)S(1)}, f32[20,4,1,128]{3,2,1,0:T(1,128)S(1)}, u32[]{:S(2)}, u32[]{:S(2)}) %collective-permute-start.7) | collective-permute-done | bytes 40992 | tf_op jit(solution)/shard_map/ppermute | solution.py:26
  43.3 2.0 %conditional.9 = (f32[20,2,16,128]{3,2,1,0:T(8,128)S(1)}, f32[2,2,16,128]{3,1,2,0:T(2,128)S(1)}) conditional(s32[]{:T(128)} %convert_element_type.24, (f32[2,16,128]{2,1,0:T(8,128)S(1)}, f32[20,4,16,128]{3,2,1,0:T(8,128)S(1)}, f32[20,4,18,128]{3,2,1,0:T(8,128)S(1)}, f32[20,2,16,128]{3,2,1,0:T(8,128)S(1)}, f32[2,2,16,128]{3,2,1,0:T(8,128)S(1)}, ...), branch_computations={%region_6.0_spmd, %region_7.0_spmd} | conditional | flops 19365888 | bytes 7598608 | solution.py:167
  45.3 3.2 %collective-permute-start.8 = (f32[20,1,16,128]{3,2,1,0:T(8,128)S(1)}, f32[20,1,16,128]{3,2,1,0:T(8,128)S(1)}, u32[]{:S(2)}, u32[]{:S(2)}) collective-permute-start(f32[20,1,16,128]{3,2,1,0:T(8,128)S(1)} %get-tuple-element.460), channel_id=1, source_target_pairs={{0,4},{4,8},{8,12},{1,5},{5,9},{9,13},{2,6},{6,10},{10,14},{3,7},{... | collective-permute-start | bytes 491528 | tf_op jit(solution)/shard_map/ppermute | solution.py:25
  50.9 4.1 %collective-permute-done.9 = f32[20,1,16,128]{3,2,1,0:T(8,128)S(1)} collective-permute-done((f32[20,1,16,128]{3,2,1,0:T(8,128)S(1)}, f32[20,1,16,128]{3,2,1,0:T(8,128)S(1)}, u32[]{:S(2)}, u32[]{:S(2)}) %collective-permute-start.9) | collective-permute-done | bytes 163872 | tf_op jit(solution)/shard_map/ppermute | solution.py:26
  55.0 3.0 %collective-permute-start.10 = (f32[20,4,1,128]{3,2,1,0:T(1,128)S(1)}, f32[20,4,1,128]{3,2,1,0:T(1,128)S(1)}, u32[]{:S(2)}, u32[]{:S(2)}) collective-permute-start(f32[20,4,1,128]{3,2,1,0:T(1,128)S(1)} %get-tuple-element.449), channel_id=1, source_target_pairs={{0,1},{1,2},{2,3},{4,5},{5,6},{6,7},{8,9},{9,10},{10,11},{12,13},{... | collective-permute-start | bytes 122888 | tf_op jit(solution)/shard_map/ppermute | solution.py:25
  58.0 1.9 %collective-permute-start.11 = (f32[20,4,1,128]{3,2,1,0:T(1,128)S(1)}, f32[20,4,1,128]{3,2,1,0:T(1,128)S(1)}, u32[]{:S(2)}, u32[]{:S(2)}) collective-permute-start(f32[20,4,1,128]{3,2,1,0:T(1,128)S(1)} %get-tuple-element.450), channel_id=1, source_target_pairs={{1,0},{2,1},{3,2},{5,4},{6,5},{7,6},{9,8},{10,9},{11,10},{13,12},{... | collective-permute-start | bytes 122888 | tf_op jit(solution)/shard_map/ppermute | solution.py:26
  60.0 3.4 %collective-permute-done.11 = f32[20,4,1,128]{3,2,1,0:T(1,128)S(1)} collective-permute-done((f32[20,4,1,128]{3,2,1,0:T(1,128)S(1)}, f32[20,4,1,128]{3,2,1,0:T(1,128)S(1)}, u32[]{:S(2)}, u32[]{:S(2)}) %collective-permute-start.11) | collective-permute-done | bytes 40992 | tf_op jit(solution)/shard_map/ppermute | solution.py:26
  63.5 2.2 %conditional.10 = (f32[20,2,16,128]{3,2,1,0:T(8,128)S(1)}, f32[2,2,16,128]{3,1,2,0:T(2,128)S(1)}) conditional(s32[]{:T(128)} %convert_element_type.24, (f32[2,16,128]{2,1,0:T(8,128)S(1)}, f32[20,4,16,128]{3,2,1,0:T(8,128)S(1)}, f32[20,4,18,128]{3,2,1,0:T(8,128)S(1)}, f32[20,2,16,128]{3,2,1,0:T(8,128)S(1)}, f32[2,2,16,128]{3,2,1,0:T(8,128)S(1)}, ...), branch_computations={%region_9.0_spmd, %region_10.0_spmd} | conditional | flops 19365888 | bytes 7598608 | solution.py:167
  65.7 1.6 %collective-permute-start.12 = (f32[20,1,16,128]{3,2,1,0:T(8,128)S(1)}, f32[20,1,16,128]{3,2,1,0:T(8,128)S(1)}, u32[]{:S(2)}, u32[]{:S(2)}) collective-permute-start(f32[20,1,16,128]{3,2,1,0:T(8,128)S(1)} %get-tuple-element.458), channel_id=1, source_target_pairs={{0,4},{4,8},{8,12},{1,5},{5,9},{9,13},{2,6},{6,10},{10,14},{3,7},{... | collective-permute-start | bytes 491528 | tf_op jit(solution)/shard_map/ppermute | solution.py:25
  67.4 1.3 %collective-permute-start.13 = (f32[20,1,16,128]{3,2,1,0:T(8,128)S(1)}, f32[20,1,16,128]{3,2,1,0:T(8,128)S(1)}, u32[]{:S(2)}, u32[]{:S(2)}) collective-permute-start(f32[20,1,16,128]{3,2,1,0:T(8,128)S(1)} %get-tuple-element.457), channel_id=1, source_target_pairs={{4,0},{8,4},{12,8},{5,1},{9,5},{13,9},{6,2},{10,6},{14,10},{7,3},{... | collective-permute-start | bytes 491528 | tf_op jit(solution)/shard_map/ppermute | solution.py:26
  69.7 4.1 %collective-permute-done.13 = f32[20,1,16,128]{3,2,1,0:T(8,128)S(1)} collective-permute-done((f32[20,1,16,128]{3,2,1,0:T(8,128)S(1)}, f32[20,1,16,128]{3,2,1,0:T(8,128)S(1)}, u32[]{:S(2)}, u32[]{:S(2)}) %collective-permute-start.13) | collective-permute-done | bytes 163872 | tf_op jit(solution)/shard_map/ppermute | solution.py:26
  73.8 3.0 %collective-permute-start.14 = (f32[20,4,1,128]{3,2,1,0:T(1,128)S(1)}, f32[20,4,1,128]{3,2,1,0:T(1,128)S(1)}, u32[]{:S(2)}, u32[]{:S(2)}) collective-permute-start(f32[20,4,1,128]{3,2,1,0:T(1,128)S(1)} %get-tuple-element.447), channel_id=1, source_target_pairs={{0,1},{1,2},{2,3},{4,5},{5,6},{6,7},{8,9},{9,10},{10,11},{12,13},{... | collective-permute-start | bytes 122888 | tf_op jit(solution)/shard_map/ppermute | solution.py:25
  76.9 1.9 %collective-permute-start.15 = (f32[20,4,1,128]{3,2,1,0:T(1,128)S(1)}, f32[20,4,1,128]{3,2,1,0:T(1,128)S(1)}, u32[]{:S(2)}, u32[]{:S(2)}) collective-permute-start(f32[20,4,1,128]{3,2,1,0:T(1,128)S(1)} %get-tuple-element.448), channel_id=1, source_target_pairs={{1,0},{2,1},{3,2},{5,4},{6,5},{7,6},{9,8},{10,9},{11,10},{13,12},{... | collective-permute-start | bytes 122888 | tf_op jit(solution)/shard_map/ppermute | solution.py:26
  78.8 3.4 %collective-permute-done.15 = f32[20,4,1,128]{3,2,1,0:T(1,128)S(1)} collective-permute-done((f32[20,4,1,128]{3,2,1,0:T(1,128)S(1)}, f32[20,4,1,128]{3,2,1,0:T(1,128)S(1)}, u32[]{:S(2)}, u32[]{:S(2)}) %collective-permute-start.15) | collective-permute-done | bytes 40992 | tf_op jit(solution)/shard_map/ppermute | solution.py:26
  82.4 2.0 %conditional.11 = (f32[20,2,16,128]{3,2,1,0:T(8,128)S(1)}, f32[2,2,16,128]{3,1,2,0:T(2,128)S(1)}) conditional(s32[]{:T(128)} %convert_element_type.24, (f32[2,16,128]{2,1,0:T(8,128)S(1)}, f32[20,4,16,128]{3,2,1,0:T(8,128)S(1)}, f32[20,4,18,128]{3,2,1,0:T(8,128)S(1)}, f32[20,2,16,128]{3,2,1,0:T(8,128)S(1)}, f32[2,2,16,128]{3,2,1,0:T(8,128)S(1)}, ...), branch_computations={%region_12.0_spmd, %region_13.0_spmd} | conditional | flops 19365888 | bytes 7598608 | solution.py:167
  84.4 1.6 %collective-permute-start.16 = (f32[20,1,16,128]{3,2,1,0:T(8,128)S(1)}, f32[20,1,16,128]{3,2,1,0:T(8,128)S(1)}, u32[]{:S(2)}, u32[]{:S(2)}) collective-permute-start(f32[20,1,16,128]{3,2,1,0:T(8,128)S(1)} %get-tuple-element.456), channel_id=1, source_target_pairs={{0,4},{4,8},{8,12},{1,5},{5,9},{9,13},{2,6},{6,10},{10,14},{3,7},{... | collective-permute-start | bytes 491528 | tf_op jit(solution)/shard_map/ppermute | solution.py:25
  88.9 3.5 %collective-permute-done.17 = f32[20,1,16,128]{3,2,1,0:T(8,128)S(1)} collective-permute-done((f32[20,1,16,128]{3,2,1,0:T(8,128)S(1)}, f32[20,1,16,128]{3,2,1,0:T(8,128)S(1)}, u32[]{:S(2)}, u32[]{:S(2)}) %collective-permute-start.17) | collective-permute-done | bytes 163872 | tf_op jit(solution)/shard_map/ppermute | solution.py:26
  92.5 3.0 %collective-permute-start.18 = (f32[20,4,1,128]{3,2,1,0:T(1,128)S(1)}, f32[20,4,1,128]{3,2,1,0:T(1,128)S(1)}, u32[]{:S(2)}, u32[]{:S(2)}) collective-permute-start(f32[20,4,1,128]{3,2,1,0:T(1,128)S(1)} %get-tuple-element.445), channel_id=1, source_target_pairs={{0,1},{1,2},{2,3},{4,5},{5,6},{6,7},{8,9},{9,10},{10,11},{12,13},{... | collective-permute-start | bytes 122888 | tf_op jit(solution)/shard_map/ppermute | solution.py:25
  95.5 1.9 %collective-permute-start.19 = (f32[20,4,1,128]{3,2,1,0:T(1,128)S(1)}, f32[20,4,1,128]{3,2,1,0:T(1,128)S(1)}, u32[]{:S(2)}, u32[]{:S(2)}) collective-permute-start(f32[20,4,1,128]{3,2,1,0:T(1,128)S(1)} %get-tuple-element.446), channel_id=1, source_target_pairs={{1,0},{2,1},{3,2},{5,4},{6,5},{7,6},{9,8},{10,9},{11,10},{13,12},{... | collective-permute-start | bytes 122888 | tf_op jit(solution)/shard_map/ppermute | solution.py:26
  98.8 2.1 %collective-permute-done.19 = f32[20,4,1,128]{3,2,1,0:T(1,128)S(1)} collective-permute-done((f32[20,4,1,128]{3,2,1,0:T(1,128)S(1)}, f32[20,4,1,128]{3,2,1,0:T(1,128)S(1)}, u32[]{:S(2)}, u32[]{:S(2)}) %collective-permute-start.19) | collective-permute-done | bytes 40992 | tf_op jit(solution)/shard_map/ppermute | solution.py:26
  102.1 2.0 %conditional.13 = (f32[1,20,2,16,128]{4,3,2,1,0:T(8,128)S(1)}) conditional(s32[]{:T(128)} %convert_element_type.24, (f32[2,16,128]{2,1,0:T(8,128)S(1)}, f32[20,4,16,128]{3,2,1,0:T(8,128)S(1)}, f32[20,4,18,128]{3,2,1,0:T(8,128)S(1)}, f32[20,2,16,128]{3,2,1,0:T(8,128)S(1)}, f32[2,2,16,128]{3,2,1,0:T(8,128)S(1)}, /*index=5*/f32[19]{0:T(128)S(1)}, ...), branch_computations={%region_17.18_spmd, %region_18.19_spmd} | conditional | flops 19365888 | bytes 7598600 | solution.py:167
  (106 shorter events, 26.9 us)
Async XLA Ops:
  0.0 0.8 copy-start.2
  2.0 6.1 %collective-permute-start = (f32[20,1,16,128]{3,2,1,0:T(8,128)S(1)}, f32[20,1,16,128]{3,2,1,0:T(8,128)S(1)}, u32[]{:S(2)}, u32[]{:S(2)}) collective-permute-start(f32[20,1,16,128]{3,2,1,0:T(8,128)S(1)} %get-tuple-element.463), channel_id=1, source_target_pairs={{0,4},{4,8},{8,12},{1,5},{5,9},{9,13},{2,6},{6,10},{10,14},{3,7},{... | collective-permute-start | bytes 491528 | tf_op jit(solution)/shard_map/ppermute | solution.py:25
  5.3 6.6 %collective-permute-start.1 = (f32[20,1,16,128]{3,2,1,0:T(8,128)S(1)}, f32[20,1,16,128]{3,2,1,0:T(8,128)S(1)}, u32[]{:S(2)}, u32[]{:S(2)}) collective-permute-start(f32[20,1,16,128]{3,2,1,0:T(8,128)S(1)} %get-tuple-element.464), channel_id=1, source_target_pairs={{4,0},{8,4},{12,8},{5,1},{9,5},{13,9},{6,2},{10,6},{14,10},{7,3},{... | collective-permute-start | bytes 491528 | tf_op jit(solution)/shard_map/ppermute | solution.py:26
  12.0 6.8 %copy-start.4 = (s32[19]{0:T(128)S(1)}, s32[19]{0:T(128)}, u32[]{:S(2)}) copy-start(s32[19]{0:T(128)} %param.22) | copy-start | bytes 232
  12.0 6.9 %collective-permute-start.2 = (f32[20,4,1,128]{3,2,1,0:T(1,128)S(1)}, f32[20,4,1,128]{3,2,1,0:T(1,128)S(1)}, u32[]{:S(2)}, u32[]{:S(2)}) collective-permute-start(f32[20,4,1,128]{3,2,1,0:T(1,128)S(1)} %get-tuple-element.453), channel_id=1, source_target_pairs={{0,1},{1,2},{2,3},{4,5},{5,6},{6,7},{8,9},{9,10},{10,11},{12,13},{... | collective-permute-start | bytes 122888 | tf_op jit(solution)/shard_map/ppermute | solution.py:25
  17.0 5.3 %collective-permute-start.3 = (f32[20,4,1,128]{3,2,1,0:T(1,128)S(1)}, f32[20,4,1,128]{3,2,1,0:T(1,128)S(1)}, u32[]{:S(2)}, u32[]{:S(2)}) collective-permute-start(f32[20,4,1,128]{3,2,1,0:T(1,128)S(1)} %get-tuple-element.454), channel_id=1, source_target_pairs={{1,0},{2,1},{3,2},{5,4},{6,5},{7,6},{9,8},{10,9},{11,10},{13,12},{... | collective-permute-start | bytes 122888 | tf_op jit(solution)/shard_map/ppermute | solution.py:26
  19.0 3.5 %copy-start = (f32[2,2,16,128]{3,2,1,0:T(8,128)S(1)}, f32[2,2,16,128]{3,2,1,0:T(8,128)}, u32[]{:S(2)}) copy-start(f32[2,2,16,128]{3,2,1,0:T(8,128)} %param.21) | copy-start | bytes 98308
  22.4 0.7 copy-start.3
  25.1 5.5 %collective-permute-start.4 = (f32[20,1,16,128]{3,2,1,0:T(8,128)S(1)}, f32[20,1,16,128]{3,2,1,0:T(8,128)S(1)}, u32[]{:S(2)}, u32[]{:S(2)}) collective-permute-start(f32[20,1,16,128]{3,2,1,0:T(8,128)S(1)} %get-tuple-element.462), channel_id=1, source_target_pairs={{0,4},{4,8},{8,12},{1,5},{5,9},{9,13},{2,6},{6,10},{10,14},{3,7},{... | collective-permute-start | bytes 491528 | tf_op jit(solution)/shard_map/ppermute | solution.py:25
  28.3 6.4 %collective-permute-start.5 = (f32[20,1,16,128]{3,2,1,0:T(8,128)S(1)}, f32[20,1,16,128]{3,2,1,0:T(8,128)S(1)}, u32[]{:S(2)}, u32[]{:S(2)}) collective-permute-start(f32[20,1,16,128]{3,2,1,0:T(8,128)S(1)} %get-tuple-element.461), channel_id=1, source_target_pairs={{4,0},{8,4},{12,8},{5,1},{9,5},{13,9},{6,2},{10,6},{14,10},{7,3},{... | collective-permute-start | bytes 491528 | tf_op jit(solution)/shard_map/ppermute | solution.py:26
  34.8 5.0 %collective-permute-start.6 = (f32[20,4,1,128]{3,2,1,0:T(1,128)S(1)}, f32[20,4,1,128]{3,2,1,0:T(1,128)S(1)}, u32[]{:S(2)}, u32[]{:S(2)}) collective-permute-start(f32[20,4,1,128]{3,2,1,0:T(1,128)S(1)} %get-tuple-element.451), channel_id=1, source_target_pairs={{0,1},{1,2},{2,3},{4,5},{5,6},{6,7},{8,9},{9,10},{10,11},{12,13},{... | collective-permute-start | bytes 122888 | tf_op jit(solution)/shard_map/ppermute | solution.py:25
  37.8 5.3 %collective-permute-start.7 = (f32[20,4,1,128]{3,2,1,0:T(1,128)S(1)}, f32[20,4,1,128]{3,2,1,0:T(1,128)S(1)}, u32[]{:S(2)}, u32[]{:S(2)}) collective-permute-start(f32[20,4,1,128]{3,2,1,0:T(1,128)S(1)} %get-tuple-element.452), channel_id=1, source_target_pairs={{1,0},{2,1},{3,2},{5,4},{6,5},{7,6},{9,8},{10,9},{11,10},{13,12},{... | collective-permute-start | bytes 122888 | tf_op jit(solution)/shard_map/ppermute | solution.py:26
  45.3 5.5 %collective-permute-start.8 = (f32[20,1,16,128]{3,2,1,0:T(8,128)S(1)}, f32[20,1,16,128]{3,2,1,0:T(8,128)S(1)}, u32[]{:S(2)}, u32[]{:S(2)}) collective-permute-start(f32[20,1,16,128]{3,2,1,0:T(8,128)S(1)} %get-tuple-element.460), channel_id=1, source_target_pairs={{0,4},{4,8},{8,12},{1,5},{5,9},{9,13},{2,6},{6,10},{10,14},{3,7},{... | collective-permute-start | bytes 491528 | tf_op jit(solution)/shard_map/ppermute | solution.py:25
  48.6 6.4 %collective-permute-start.9 = (f32[20,1,16,128]{3,2,1,0:T(8,128)S(1)}, f32[20,1,16,128]{3,2,1,0:T(8,128)S(1)}, u32[]{:S(2)}, u32[]{:S(2)}) collective-permute-start(f32[20,1,16,128]{3,2,1,0:T(8,128)S(1)} %get-tuple-element.459), channel_id=1, source_target_pairs={{4,0},{8,4},{12,8},{5,1},{9,5},{13,9},{6,2},{10,6},{14,10},{7,3},{... | collective-permute-start | bytes 491528 | tf_op jit(solution)/shard_map/ppermute | solution.py:26
  55.0 5.0 %collective-permute-start.10 = (f32[20,4,1,128]{3,2,1,0:T(1,128)S(1)}, f32[20,4,1,128]{3,2,1,0:T(1,128)S(1)}, u32[]{:S(2)}, u32[]{:S(2)}) collective-permute-start(f32[20,4,1,128]{3,2,1,0:T(1,128)S(1)} %get-tuple-element.449), channel_id=1, source_target_pairs={{0,1},{1,2},{2,3},{4,5},{5,6},{6,7},{8,9},{9,10},{10,11},{12,13},{... | collective-permute-start | bytes 122888 | tf_op jit(solution)/shard_map/ppermute | solution.py:25
  58.0 5.3 %collective-permute-start.11 = (f32[20,4,1,128]{3,2,1,0:T(1,128)S(1)}, f32[20,4,1,128]{3,2,1,0:T(1,128)S(1)}, u32[]{:S(2)}, u32[]{:S(2)}) collective-permute-start(f32[20,4,1,128]{3,2,1,0:T(1,128)S(1)} %get-tuple-element.450), channel_id=1, source_target_pairs={{1,0},{2,1},{3,2},{5,4},{6,5},{7,6},{9,8},{10,9},{11,10},{13,12},{... | collective-permute-start | bytes 122888 | tf_op jit(solution)/shard_map/ppermute | solution.py:26
  65.7 3.9 %collective-permute-start.12 = (f32[20,1,16,128]{3,2,1,0:T(8,128)S(1)}, f32[20,1,16,128]{3,2,1,0:T(8,128)S(1)}, u32[]{:S(2)}, u32[]{:S(2)}) collective-permute-start(f32[20,1,16,128]{3,2,1,0:T(8,128)S(1)} %get-tuple-element.458), channel_id=1, source_target_pairs={{0,4},{4,8},{8,12},{1,5},{5,9},{9,13},{2,6},{6,10},{10,14},{3,7},{... | collective-permute-start | bytes 491528 | tf_op jit(solution)/shard_map/ppermute | solution.py:25
  67.4 6.4 %collective-permute-start.13 = (f32[20,1,16,128]{3,2,1,0:T(8,128)S(1)}, f32[20,1,16,128]{3,2,1,0:T(8,128)S(1)}, u32[]{:S(2)}, u32[]{:S(2)}) collective-permute-start(f32[20,1,16,128]{3,2,1,0:T(8,128)S(1)} %get-tuple-element.457), channel_id=1, source_target_pairs={{4,0},{8,4},{12,8},{5,1},{9,5},{13,9},{6,2},{10,6},{14,10},{7,3},{... | collective-permute-start | bytes 491528 | tf_op jit(solution)/shard_map/ppermute | solution.py:26
  73.8 5.0 %collective-permute-start.14 = (f32[20,4,1,128]{3,2,1,0:T(1,128)S(1)}, f32[20,4,1,128]{3,2,1,0:T(1,128)S(1)}, u32[]{:S(2)}, u32[]{:S(2)}) collective-permute-start(f32[20,4,1,128]{3,2,1,0:T(1,128)S(1)} %get-tuple-element.447), channel_id=1, source_target_pairs={{0,1},{1,2},{2,3},{4,5},{5,6},{6,7},{8,9},{9,10},{10,11},{12,13},{... | collective-permute-start | bytes 122888 | tf_op jit(solution)/shard_map/ppermute | solution.py:25
  76.9 5.3 %collective-permute-start.15 = (f32[20,4,1,128]{3,2,1,0:T(1,128)S(1)}, f32[20,4,1,128]{3,2,1,0:T(1,128)S(1)}, u32[]{:S(2)}, u32[]{:S(2)}) collective-permute-start(f32[20,4,1,128]{3,2,1,0:T(1,128)S(1)} %get-tuple-element.448), channel_id=1, source_target_pairs={{1,0},{2,1},{3,2},{5,4},{6,5},{7,6},{9,8},{10,9},{11,10},{13,12},{... | collective-permute-start | bytes 122888 | tf_op jit(solution)/shard_map/ppermute | solution.py:26
  84.4 4.5 %collective-permute-start.16 = (f32[20,1,16,128]{3,2,1,0:T(8,128)S(1)}, f32[20,1,16,128]{3,2,1,0:T(8,128)S(1)}, u32[]{:S(2)}, u32[]{:S(2)}) collective-permute-start(f32[20,1,16,128]{3,2,1,0:T(8,128)S(1)} %get-tuple-element.456), channel_id=1, source_target_pairs={{0,4},{4,8},{8,12},{1,5},{5,9},{9,13},{2,6},{6,10},{10,14},{3,7},{... | collective-permute-start | bytes 491528 | tf_op jit(solution)/shard_map/ppermute | solution.py:25
  86.1 6.4 %collective-permute-start.17 = (f32[20,1,16,128]{3,2,1,0:T(8,128)S(1)}, f32[20,1,16,128]{3,2,1,0:T(8,128)S(1)}, u32[]{:S(2)}, u32[]{:S(2)}) collective-permute-start(f32[20,1,16,128]{3,2,1,0:T(8,128)S(1)} %get-tuple-element.455), channel_id=1, source_target_pairs={{4,0},{8,4},{12,8},{5,1},{9,5},{13,9},{6,2},{10,6},{14,10},{7,3},{... | collective-permute-start | bytes 491528 | tf_op jit(solution)/shard_map/ppermute | solution.py:26
  87.6 13.4 %collective-permute-start.21 = (f32[1,2,16,128]{3,1,2,0:T(2,128)S(1)}, f32[1,2,16,128]{3,1,2,0:T(2,128)S(1)}, u32[]{:S(2)}, u32[]{:S(2)}) collective-permute-start(f32[1,2,16,128]{3,1,2,0:T(2,128)S(1)} %bitcast.185), channel_id=1, source_target_pairs={{16,0},{17,1},{18,2},{19,3},{20,4},{21,5},{22,6},{23,7},{24,8},{25... | collective-permute-start | bytes 49160 | tf_op jit(solution)/shard_map/ppermute | solution.py:34
  92.5 6.3 %collective-permute-start.18 = (f32[20,4,1,128]{3,2,1,0:T(1,128)S(1)}, f32[20,4,1,128]{3,2,1,0:T(1,128)S(1)}, u32[]{:S(2)}, u32[]{:S(2)}) collective-permute-start(f32[20,4,1,128]{3,2,1,0:T(1,128)S(1)} %get-tuple-element.445), channel_id=1, source_target_pairs={{0,1},{1,2},{2,3},{4,5},{5,6},{6,7},{8,9},{9,10},{10,11},{12,13},{... | collective-permute-start | bytes 122888 | tf_op jit(solution)/shard_map/ppermute | solution.py:25
  95.5 5.3 %collective-permute-start.19 = (f32[20,4,1,128]{3,2,1,0:T(1,128)S(1)}, f32[20,4,1,128]{3,2,1,0:T(1,128)S(1)}, u32[]{:S(2)}, u32[]{:S(2)}) collective-permute-start(f32[20,4,1,128]{3,2,1,0:T(1,128)S(1)} %get-tuple-element.446), channel_id=1, source_target_pairs={{1,0},{2,1},{3,2},{5,4},{6,5},{7,6},{9,8},{10,9},{11,10},{13,12},{... | collective-permute-start | bytes 122888 | tf_op jit(solution)/shard_map/ppermute | solution.py:26
  97.5 4.7 %collective-permute-start.20 = (f32[2,2,16,128]{3,2,1,0:T(8,128)S(1)}, f32[2,2,16,128]{3,2,1,0:T(8,128)S(1)}, u32[]{:S(2)}, u32[]{:S(2)}) collective-permute-start(f32[2,2,16,128]{3,2,1,0:T(8,128)S(1)} %copy_multiply_fusion), channel_id=1, source_target_pairs={{0,16},{1,17},{2,18},{3,19},{4,20},{5,21},{6,22},{7,23},{8,24},{9,... | collective-permute-start | bytes 98312 | tf_op jit(solution)/shard_map/ppermute | solution.py:34
  104.1 0.7 copy-start.1
where the time goes:
time: 107 us; the launch traced here: 105 us
  starting transfers between devices  48.6 us (45%)
  waiting for transfers between devices  40.2 us (38%)
  local copies, waits for them, and re-layouts  7.7 us (7%)
  other arithmetic  4.6 us (4%)
  matrix products  2.7 us (3%)
    ppermute x10, waiting for transfers between devices, extended_2(): after = lax.ppermute(leading, axis, down)  35 us
    ppermute x10, starting transfers between devices, extended_2(): before = lax.ppermute(last, axis, up)  29.9 us
    ppermute x10, starting transfers between devices, extended_2(): after = lax.ppermute(leading, axis, down)  16.1 us
    another operation x19, local copies, waits for them, and re-layouts  5.39 us
    ppermute x10, waiting for transfers between devices, extended_2(): before = lax.ppermute(last, axis, up)  4.12 us
    ppermute x2, starting transfers between devices, from_behind(): return lax.ppermute(shard, axis, pairs)  2.58 us
    dot_general x5, matrix products, tracer_substep(): jnp.einsum('ts,sxyk->txyk', onehot, living, precision=lax.Precision.HIGHEST)  2.52 us
  transfers between devices with their start and end apart: 22, of which 15 were waited for; matrix products, arithmetic and copies ran while one was open for 1% of the time, Pallas kernels for 0%

commit v1 on v0

v1 whole, which is shorter than its diff:
```python
import jax
import jax.numpy as jnp
from jax import lax
from jax.experimental import pallas as pl
from jax.experimental.pallas import tpu as pltpu
from jax.sharding import PartitionSpec as P

NSUB = 4
STEPS = NSUB + 1
DT = 0.1
NU = 1.0
CORIOLIS = 0.5
DRAG = 0.1
MORTALITY = 0.1
HEATING = 2.0
SURFACE = 8.0
MESH = pl.DeviceIdType.MESH
WEST, EAST, SOUTH, NORTH = 0, 1, 2, 3


def kernel(
    state_hbm, levels_ref, flux_hbm, prey_ref, rate_ref, out_hbm,
    raw, cur, tanhs, hx, ys, yr, wet, flux, run, light, heat,
    load_sem, flux_sem, store_sem, send_sem, recv_sem, pair_send, pair_recv,
):
    groups = cur.shape[1]
    size_x, size_y, depth = cur.shape[3:]
    last_x, last_y = size_x - 1, size_y - 1
    species = prey_ref.shape[0]
    half = lax.axis_index("half")
    gx, gy = lax.axis_index("gx"), lax.axis_index("gy")
    nx, ny = lax.axis_size("gx"), lax.axis_size("gy")
    is_ocean = half == 0
    has = (gx > 0, gx < nx - 1, gy > 0, gy < ny - 1)
    peer = ({"gx": gx - 1}, {"gx": gx + 1}, {"gy": gy - 1}, {"gy": gy + 1})
    partner = {"half": 1 - half}

    def load(g):
        return pltpu.make_async_copy(state_hbm.at[0, pl.ds(4 * g, 4)], raw.at[g], load_sem.at[g])

    def store(g):
        return pltpu.make_async_copy(
            cur.at[STEPS, g], out_hbm.at[0, pl.ds(4 * g, 4)], store_sem.at[g]
        )

    flux_load = pltpu.make_async_copy(flux_hbm, flux.at[0], flux_sem)
    for g in range(groups):
        load(g).start()
    flux_load.start()

    barrier = pltpu.get_barrier_semaphore()
    for side in range(4):
        @pl.when(has[side])
        def _():
            pl.semaphore_signal(barrier, inc=1, device_id=peer[side], device_id_type=MESH)
    pl.semaphore_signal(barrier, inc=1, device_id=partner, device_id_type=MESH)

    for side in (WEST, EAST):
        @pl.when(jnp.logical_not(has[side]))
        def _():
            for s in range(STEPS):
                hx[s, side] = jnp.zeros(hx.shape[2:], jnp.float32)
    for side in (SOUTH, NORTH):
        @pl.when(jnp.logical_not(has[side]))
        def _():
            for s in range(STEPS):
                yr[s, side - 2] = jnp.zeros(yr.shape[2:], jnp.float32)

    rows = lax.broadcasted_iota(jnp.int32, (size_y, depth), 0)
    level_k = lax.broadcasted_iota(jnp.int32, (size_y, depth), 1).astype(jnp.float32)
    diagonal = lax.broadcasted_iota(jnp.int32, (size_y, size_y), 0) == lax.broadcasted_iota(
        jnp.int32, (size_y, size_y), 1
    )
    for i in range(size_x):
        active = []
        for c in range(4):
            line = levels_ref[c, pl.ds(i, 1), :].astype(jnp.float32)
            spread = jnp.where(diagonal, jnp.broadcast_to(line, (size_y, size_y)), 0.0)
            active.append(jnp.sum(spread, axis=1, keepdims=True))
        most = jnp.maximum(jnp.maximum(active[0], active[1]), jnp.maximum(active[2], active[3]))
        for c in range(4):
            mine = jnp.where(is_ocean, active[c], most)
            wet[c, i] = jnp.where(level_k < mine, 1.0, 0.0)

    run[...] = jnp.zeros(run.shape, jnp.float32)
    heat[...] = jnp.zeros(heat.shape, jnp.float32)

    def x_copy(s, g, side, ocean):
        row = 0 if side == WEST else last_x
        if ocean:
            channels = pl.ds(0, 2) if side == WEST else pl.ds(2, 2)
            src = cur.at[s, g, channels, row]
            dst = hx.at[s, 1 - side, g, pl.ds(0, 2)]
        else:
            src = cur.at[s, g, :, row]
            dst = hx.at[s, 1 - side, g]
        return pltpu.make_async_remote_copy(
            src, dst, send_sem.at[s, g, side], recv_sem.at[s, g, 1 - side],
            device_id=peer[side], device_id_type=MESH,
        )

    def y_copy(s, g, side):
        return pltpu.make_async_remote_copy(
            ys.at[s, side - 2, g], yr.at[s, 3 - side, g],
            send_sem.at[s, g, side], recv_sem.at[s, g, 5 - side],
            device_id=peer[side], device_id_type=MESH,
        )

    def copy_of(s, g, side, ocean):
        return x_copy(s, g, side, ocean) if side < 2 else y_copy(s, g, side)

    def start_copies(s, g, ocean):
        for side in range(4):
            @pl.when(has[side])
            def _():
                copy_of(s, g, side, ocean).start()

    def wait_arrivals(s, g, ocean):
        for side in range(4):
            @pl.when(has[side])
            def _():
                if side < 2:
                    lands = hx.at[s, side, g, pl.ds(0, 2)] if ocean else hx.at[s, side, g]
                else:
                    lands = yr.at[s, side - 2, g]
                pltpu.make_async_remote_copy(
                    lands, lands, send_sem.at[s, g, side], recv_sem.at[s, g, side],
                    device_id=peer[side], device_id_type=MESH,
                ).wait_recv()

    def wait_sends(ocean):
        def step(s, carry):
            def group(g, inner):
                for side in range(4):
                    @pl.when(has[side])
                    def _():
                        copy_of(s, g, side, ocean).wait_send()
                return inner
            return lax.fori_loop(0, groups, group, carry)
        lax.fori_loop(0, STEPS, step, 0)

    def put(s, g, c, i, value):
        cur[s, g, c, i] = value
        ys[s, 0, g, pl.ds(c * size_x + i, 1), :] = value[0:1]
        ys[s, 1, g, pl.ds(c * size_x + i, 1), :] = value[last_y:]

    def north_of(value, s, g, c, i):
        arrived = yr[s, 1, g, pl.ds(c * size_x + i, 1), :]
        return jnp.where(rows == last_y, arrived, pltpu.roll(value, size_y - 1, 0))

    def south_of(value, s, g, c, i):
        arrived = yr[s, 0, g, pl.ds(c * size_x + i, 1), :]
        return jnp.where(rows == 0, arrived, pltpu.roll(value, 1, 0))

    def ocean_part():
        def first(g, carry):
            load(g).wait()
            for c in range(4):
                for i in range(size_x):
                    put(0, g, c, i, raw[g, c, i] * wet[c, i])
            start_copies(0, g, True)
            return carry

        lax.fori_loop(0, groups, first, 0)
        flux_load.wait()

        def pair_copy():
            return pltpu.make_async_remote_copy(
                run, flux.at[1], pair_send, pair_recv, device_id=partner, device_id_type=MESH
            )

        def step(s, carry):
            def field(f, inner):
                wait_arrivals(s, f, True)

                @pl.when(jnp.logical_and(s == NSUB, f == 2))
                def _():
                    pltpu.make_async_remote_copy(
                        light, light, pair_send, pair_recv,
                        device_id=partner, device_id_type=MESH,
                    ).wait_recv()
                    heat[...] = light[...] * HEATING

                of_u = jnp.where(f == 0, -DRAG, jnp.where(f == 1, -CORIOLIS, 0.0))
                of_v = jnp.where(f == 0, CORIOLIS, jnp.where(f == 1, -DRAG, 0.0))
                of_heat = jnp.where(f == 2, 1.0, 0.0)
                ageing = jnp.where(f == 4, 1.0, 0.0)
                for i in range(size_x):
                    total = None
                    for c in range(4):
                        a, b = c // 2, c % 2
                        centre = cur[s, f, c, i]
                        if a == 0:
                            to_east = cur[s, f, 2 + b, i]
                            to_west = cur[s, f, 2 + b, i - 1] if i > 0 else hx[s, WEST, f, b]
                        else:
                            to_west = cur[s, f, b, i]
                            to_east = cur[s, f, b, i + 1] if i < last_x else hx[s, EAST, f, b]
                        other = cur[s, f, 2 * a + 1 - b, i]
                        if b == 0:
                            to_north = other
                            to_south = south_of(other, s, f, c + 1, i)
                        else:
                            to_south = other
                            to_north = north_of(other, s, f, c - 1, i)
                        u, v = cur[s, 0, c, i], cur[s, 1, c, i]
                        spread = to_east + to_west + to_north + to_south - 4.0 * centre
                        advect = u * (to_east - to_west) * 0.5 + v * (to_north - to_south) * 0.5
                        forcing = of_u * u + of_v * v + of_heat * heat[i] + ageing
                        new = wet[c, i] * (centre + DT * (NU * spread - advect + forcing))
                        put(s + 1, f, c, i, new)
                        total = new if total is None else total + new

                    @pl.when(jnp.logical_and(f < 2, s < NSUB))
                    def _():
                        run[f, i] = run[f, i] + total * (0.25 / NSUB)

                @pl.when(s < NSUB)
                def _():
                    start_copies(s + 1, f, True)

                @pl.when(jnp.logical_and(s == NSUB - 1, f == 1))
                def _():
                    pair_copy().start()

                @pl.when(s == NSUB)
                def _():
                    store(f).start()
                return inner
            return lax.fori_loop(0, groups, field, carry)

        lax.fori_loop(0, STEPS, step, 0)
        wait_sends(True)
        pair_copy().wait_send()

    def tracer_part():
        def first(g, carry):
            load(g).wait()
            for c in range(4):
                for i in range(size_x):
                    value = raw[g, c, i] * wet[c, i]
                    put(0, g, c, i, value)
                    tanhs[0, 4 * g + c, i] = jnp.tanh(value)
            start_copies(0, g, False)
            return carry

        lax.fori_loop(0, groups, first, 0)
        flux_load.wait()

        def pair_copy():
            return pltpu.make_async_remote_copy(
                heat, light, pair_send, pair_recv, device_id=partner, device_id_type=MESH
            )

        def step(s, carry):
            now, later = lax.rem(s, 2), lax.rem(s + 1, 2)
            which = s // NSUB

            @pl.when(s == NSUB)
            def _():
                pltpu.make_async_remote_copy(
                    flux.at[1], flux.at[1], pair_send, pair_recv,
                    device_id=partner, device_id_type=MESH,
                ).wait_recv()

            def group(g, inner):
                wait_arrivals(s, g, False)
                for c in range(4):
                    t = 4 * g + c
                    living = jnp.where(t < species, 1.0, 0.0)
                    slot = jnp.minimum(t, species - 1)
                    rate = rate_ref[slot] * living
                    mortality = MORTALITY * living
                    prey = prey_ref[slot]
                    for i in range(size_x):
                        centre = cur[s, g, c, i]
                        to_west = cur[s, g, c, i - 1] if i > 0 else hx[s, WEST, g, c]
                        to_east = cur[s, g, c, i + 1] if i < last_x else hx[s, EAST, g, c]
                        to_north = north_of(centre, s, g, c, i)
                        to_south = south_of(centre, s, g, c, i)
                        spread = to_east + to_west + to_north + to_south - 4.0 * centre
                        advect = (
                            flux[which, 0, i] * (to_east - to_west) * 0.5
                            + flux[which, 1, i] * (to_north - to_south) * 0.5
                        )
                        reaction = rate * centre * tanhs[now, prey, i] - mortality * centre
                        new = wet[c, i] * (centre + DT * (NU * spread - advect + reaction))
                        put(s + 1, g, c, i, new)
                        tanhs[later, t, i] = jnp.tanh(new)

                @pl.when(s < NSUB)
                def _():
                    start_copies(s + 1, g, False)

                @pl.when(jnp.logical_and(s == NSUB - 1, g == 0))
                def _():
                    above = (
                        lax.broadcasted_iota(jnp.int32, (depth, depth), 0)
                        < lax.broadcasted_iota(jnp.int32, (depth, depth), 1)
                    ).astype(jnp.float32)
                    for i in range(size_x):
                        green = cur[s + 1, 0, 0, i]
                        soft = jnp.maximum(green, 0.0) + jnp.log(1.0 + jnp.exp(-jnp.abs(green)))
                        attenuation = wet[0, i] * (0.03 + 0.05 * soft)
                        overhead = jnp.dot(
                            attenuation, above, precision=lax.Precision.HIGHEST,
                            preferred_element_type=jnp.float32,
                        )
                        heat[i] = SURFACE * jnp.exp(-overhead) * (1.0 - jnp.exp(-attenuation))
                    pair_copy().start()

                @pl.when(s == NSUB)
                def _():
                    store(g).start()
                return inner
            return lax.fori_loop(0, groups, group, carry)

        lax.fori_loop(0, STEPS, step, 0)
        wait_sends(False)
        pair_copy().wait_send()

    greeted = 1
    for side in range(4):
        greeted = greeted + has[side].astype(jnp.int32)
    pl.semaphore_wait(barrier, greeted)

    pl.when(is_ocean)(ocean_part)
    pl.when(jnp.logical_not(is_ocean))(tracer_part)
    for g in range(groups):
        store(g).wait()


def body(state, levels, old_flux, eco_prey, eco_rate):
    channels, size_x, size_y, depth = state.shape[1:]
    groups = channels // 4
    f32 = jnp.float32
    tile = (size_x, size_y, depth)
    return pl.pallas_call(
        kernel,
        out_shape=jax.ShapeDtypeStruct(state.shape, f32),
        in_specs=[
            pl.BlockSpec(memory_space=pl.ANY),
            pl.BlockSpec(memory_space=pltpu.VMEM),
            pl.BlockSpec(memory_space=pl.ANY),
            pl.BlockSpec(memory_space=pltpu.SMEM),
            pl.BlockSpec(memory_space=pltpu.SMEM),
        ],
        out_specs=pl.BlockSpec(memory_space=pl.ANY),
        scratch_shapes=[
            pltpu.VMEM((groups, 4) + tile, f32),
            pltpu.VMEM((STEPS + 1, groups, 4) + tile, f32),
            pltpu.VMEM((2, channels) + tile, f32),
            pltpu.VMEM((STEPS, 2, groups, 4, size_y, depth), f32),
            pltpu.VMEM((STEPS + 1, 2, groups, 4 * size_x, depth), f32),
            pltpu.VMEM((STEPS, 2, groups, 4 * size_x, depth), f32),
            pltpu.VMEM((4,) + tile, f32),
            pltpu.VMEM((2, 2) + tile, f32),
            pltpu.VMEM((2,) + tile, f32),
            pltpu.VMEM(tile, f32),
            pltpu.VMEM(tile, f32),
            pltpu.SemaphoreType.DMA((groups,)),
            pltpu.SemaphoreType.DMA,
            pltpu.SemaphoreType.DMA((groups,)),
            pltpu.SemaphoreType.DMA((STEPS, groups, 4)),
            pltpu.SemaphoreType.DMA((STEPS, groups, 4)),
            pltpu.SemaphoreType.DMA,
            pltpu.SemaphoreType.DMA,
        ],
        compiler_params=pltpu.CompilerParams(
            collective_id=0, has_side_effects=True, vmem_limit_bytes=24 * 1024 * 1024
        ),
    )(state, levels, old_flux, eco_prey, eco_rate)


def solution(mesh):
    placed = (
        P("half", None, "gx", "gy", None),
        P(None, "gx", "gy"),
        P(None, "gx", "gy", None),
        P(),
        P(),
    )
    return jax.shard_map(
        body,
        mesh=mesh,
        in_specs=placed,
        out_specs=P("half", None, "gx", "gy", None),
        check_vma=False,
    )
```

time: 107 us -> 30.6 us (0.29); the launches traced: 105 us -> 30.3 us
  starting transfers between devices: 48.6 us -> 0 us
  waiting for transfers between devices: 40.2 us -> 0 us
  Pallas kernels: 0 us -> 25.8 us
  other arithmetic: 4.6 us -> 0 us
  local copies, waits for them, and re-layouts: 7.7 us -> 4.45 us
  matrix products: 2.7 us -> 0 us
    ppermute x22 -> x0, starting transfers between devices: 48.6 us -> none  [the longest x10 29.9 us: extended_2(): before = lax.ppermute(last, axis, up)]
    ppermute x22 -> x0, waiting for transfers between devices: 40.2 us -> none  [the longest x10 35 us: extended_2(): after = lax.ppermute(leading, axis, down)]
    pallas_call x0 -> x1, Pallas kernels: none -> 25.8 us  [body(): pl.pallas_call(kernel, out_shape=jax.ShapeDtypeStruct(state.shape, f32),...]
    another operation x19 -> x0, local copies, waits for them, and re-layouts: 5.39 us -> none
    unnamed x18 -> x11, local copies, waits for them, and re-layouts: 1.52 us -> 4.45 us
    dot_general x6 -> x0, matrix products: 2.7 us -> none  [the longest x5 2.52 us: tracer_substep(): jnp.einsum('ts,sxyk->txyk', onehot, living, precision=lax.Precision.HIGHEST)]
    mul x5 -> x0, other arithmetic: 2.31 us -> none  [the longest x4 1.29 us: tracer_substep(): return wet_mask * (centre + DT * (NU * spread - advect + reaction))]
    convert_element_type x5 -> x0, other arithmetic: 1.09 us -> none  [the longest x3 1.01 us: wet_of(): (lax.broadcasted_iota(jnp.int32, shape, len(shape) - 1) < levels[..., Non...]
  transfers between devices with their start and end apart: 22 -> 0, of which waited for: 15 -> 0; matrix products, arithmetic and copies ran while one was open for 1% -> 0% of each run, Pallas kernels for 0% -> 0%
where the time goes in v1:
time: 30.6 us; the launch traced here: 30.3 us
  Pallas kernels  25.8 us (84%)
  local copies, waits for them, and re-layouts  4.45 us (15%)
    pallas_call x1, Pallas kernels, body(): pl.pallas_call(kernel, out_shape=jax.ShapeDtypeStruct(state.shape, f32),...  25.8 us
    unnamed x11, local copies, waits for them, and re-layouts  4.45 us

profile of v1, /device:TPU:3, one launch (start us, length us, event | category | flops | bytes accessed | tf_op | source)
XLA Modules:
  0.0 30.3 jit_solution(8759644875902398704)
XLA Ops:
  0.0 0.0 copy-start
  0.0 1.0 %copy-done = f32[1,20,2,16,128]{4,3,2,1,0:T(8,128)S(1)} copy-done((f32[1,20,2,16,128]{4,3,2,1,0:T(8,128)S(1)}, f32[1,20,2,16,128]{4,3,2,1,0:T(8,128)}, u32[]{:S(2)}) %copy-start) | copy-done | bytes 327704
  1.0 0.0 copy-start.1
  1.0 0.8 %copy-done.1 = f32[2,2,16,128]{3,2,1,0:T(8,128)S(1)} copy-done((f32[2,2,16,128]{3,2,1,0:T(8,128)S(1)}, f32[2,2,16,128]{3,2,1,0:T(8,128)}, u32[]{:S(2)}) %copy-start.1) | copy-done | bytes 32792
  1.7 0.0 copy-start.2
  1.7 0.7 %copy-done.2 = s32[4,2,16]{2,1,0:T(2,128)S(1)} copy-done((s32[4,2,16]{2,1,0:T(2,128)S(1)}, s32[4,2,16]{2,1,0:T(2,128)}, u32[]{:S(2)}) %copy-start.2) | copy-done | bytes 536
  2.4 0.0 copy-start.3
  2.4 0.7 %copy-done.3 = s32[19]{0:T(128)S(1)} copy-done((s32[19]{0:T(128)S(1)}, s32[19]{0:T(128)}, u32[]{:S(2)}) %copy-start.3) | copy-done | bytes 100
  3.1 0.0 copy-start.4
  3.1 0.7 %copy-done.4 = f32[19]{0:T(128)S(1)} copy-done((f32[19]{0:T(128)S(1)}, f32[19]{0:T(128)}, u32[]{:S(2)}) %copy-start.4) | copy-done | bytes 100
  3.7 25.8 %shard_map.55 = f32[1,20,2,16,128]{4,3,2,1,0:T(8,128)S(1)} custom-call(f32[1,20,2,16,128]{4,3,2,1,0:T(8,128)S(1)} %copy-done, s32[4,2,16]{2,1,0:T(2,128)S(1)} %copy-done.2, f32[2,2,16,128]{3,2,1,0:T(8,128)S(1)} %copy-done.1, s32[19]{0:T(128)S(1)} %copy-done.3, f32[19]{0:T(128)S(1)} %copy-done.4), custom_call_target="tpu_custom_call" | custom-call | tf_op jit(solution)/shard_map/pallas_call | solution.py:338
  29.6 0.7 %copy.7 = f32[1,20,2,16,128]{4,3,2,1,0:T(8,128)} copy(f32[1,20,2,16,128]{4,3,2,1,0:T(8,128)S(1)} %shard_map.55) | data formatting | bytes 655360
Async XLA Ops:
  0.0 1.0 %copy-start = (f32[1,20,2,16,128]{4,3,2,1,0:T(8,128)S(1)}, f32[1,20,2,16,128]{4,3,2,1,0:T(8,128)}, u32[]{:S(2)}) copy-start(f32[1,20,2,16,128]{4,3,2,1,0:T(8,128)} %state_hbm.1) | copy-start | bytes 983044
  1.0 0.8 %copy-start.1 = (f32[2,2,16,128]{3,2,1,0:T(8,128)S(1)}, f32[2,2,16,128]{3,2,1,0:T(8,128)}, u32[]{:S(2)}) copy-start(f32[2,2,16,128]{3,2,1,0:T(8,128)} %flux_hbm.1) | copy-start | bytes 98308
  1.7 0.7 %copy-start.2 = (s32[4,2,16]{2,1,0:T(2,128)S(1)}, s32[4,2,16]{2,1,0:T(2,128)}, u32[]{:S(2)}) copy-start(s32[4,2,16]{2,1,0:T(2,128)} %levels_ref.1) | copy-start | bytes 1540
  2.4 0.7 %copy-start.3 = (s32[19]{0:T(128)S(1)}, s32[19]{0:T(128)}, u32[]{:S(2)}) copy-start(s32[19]{0:T(128)} %prey_ref.1) | copy-start | bytes 232
  3.1 0.7 %copy-start.4 = (f32[19]{0:T(128)S(1)}, f32[19]{0:T(128)}, u32[]{:S(2)}) copy-start(f32[19]{0:T(128)} %rate_ref.1) | copy-start | bytes 232

commit v2 on v1

--- a/solution.py
+++ b/solution.py
@@ -19,9 +19,9 @@
 
 
 def kernel(
-    state_hbm, levels_ref, flux_hbm, prey_ref, rate_ref, out_hbm,
-    raw, cur, tanhs, hx, ys, yr, wet, flux, run, light, heat,
-    load_sem, flux_sem, store_sem, send_sem, recv_sem, pair_send, pair_recv,
+    state_hbm, levels_hbm, flux_hbm, prey_hbm, rate_hbm, out_hbm,
+    levels_ref, prey_ref, rate_ref, raw, cur, tanhs, hx, ys, yr, wet, flux, run, light, heat,
+    load_sem, small_sem, store_sem, send_sem, recv_sem, pair_send, pair_recv,
 ):
     groups = cur.shape[1]
     size_x, size_y, depth = cur.shape[3:]
@@ -43,10 +43,16 @@
             cur.at[STEPS, g], out_hbm.at[0, pl.ds(4 * g, 4)], store_sem.at[g]
         )
 
-    flux_load = pltpu.make_async_copy(flux_hbm, flux.at[0], flux_sem)
+    levels_load = pltpu.make_async_copy(levels_hbm, levels_ref, small_sem.at[0])
+    flux_load = pltpu.make_async_copy(flux_hbm, flux.at[0], small_sem.at[1])
+    prey_load = pltpu.make_async_copy(prey_hbm, prey_ref, small_sem.at[2])
+    rate_load = pltpu.make_async_copy(rate_hbm, rate_ref, small_sem.at[3])
+    levels_load.start()
     for g in range(groups):
         load(g).start()
     flux_load.start()
+    prey_load.start()
+    rate_load.start()
 
     barrier = pltpu.get_barrier_semaphore()
     for side in range(4):
@@ -71,6 +77,7 @@
     diagonal = lax.broadcasted_iota(jnp.int32, (size_y, size_y), 0) == lax.broadcasted_iota(
         jnp.int32, (size_y, size_y), 1
     )
+    levels_load.wait()
     for i in range(size_x):
         active = []
         for c in range(4):
@@ -163,6 +170,8 @@
 
         lax.fori_loop(0, groups, first, 0)
         flux_load.wait()
+        prey_load.wait()
+        rate_load.wait()
 
         def pair_copy():
             return pltpu.make_async_remote_copy(
@@ -246,6 +255,8 @@
 
         lax.fori_loop(0, groups, first, 0)
         flux_load.wait()
+        prey_load.wait()
+        rate_load.wait()
 
         def pair_copy():
             return pltpu.make_async_remote_copy(
@@ -338,15 +349,12 @@
     return pl.pallas_call(
         kernel,
         out_shape=jax.ShapeDtypeStruct(state.shape, f32),
-        in_specs=[
-            pl.BlockSpec(memory_space=pl.ANY),
-            pl.BlockSpec(memory_space=pltpu.VMEM),
-            pl.BlockSpec(memory_space=pl.ANY),
-            pl.BlockSpec(memory_space=pltpu.SMEM),
-            pl.BlockSpec(memory_space=pltpu.SMEM),
-        ],
+        in_specs=[pl.BlockSpec(memory_space=pl.ANY)] * 5,
         out_specs=pl.BlockSpec(memory_space=pl.ANY),
         scratch_shapes=[
+            pltpu.VMEM(levels.shape, levels.dtype),
+            pltpu.SMEM(eco_prey.shape, eco_prey.dtype),
+            pltpu.SMEM(eco_rate.shape, eco_rate.dtype),
             pltpu.VMEM((groups, 4) + tile, f32),
             pltpu.VMEM((STEPS + 1, groups, 4) + tile, f32),
             pltpu.VMEM((2, channels) + tile, f32),
@@ -359,7 +367,7 @@
             pltpu.VMEM(tile, f32),
             pltpu.VMEM(tile, f32),
             pltpu.SemaphoreType.DMA((groups,)),
-            pltpu.SemaphoreType.DMA,
+            pltpu.SemaphoreType.DMA((4,)),
             pltpu.SemaphoreType.DMA((groups,)),
             pltpu.SemaphoreType.DMA((STEPS, groups, 4)),
             pltpu.SemaphoreType.DMA((STEPS, groups, 4)),
@@ -367,7 +375,7 @@
             pltpu.SemaphoreType.DMA,
         ],
         compiler_params=pltpu.CompilerParams(
-            collective_id=0, has_side_effects=True, vmem_limit_bytes=24 * 1024 * 1024
+            collective_id=0, has_side_effects=True, vmem_limit_bytes=60 * 1024 * 1024
         ),
     )(state, levels, old_flux, eco_prey, eco_rate)
 

time: 30.6 us -> 27 us (0.88)
  local copies, waits for them, and re-layouts: 4.45 us -> 1.72 us
  Pallas kernels: 25.8 us -> 25 us
    unnamed x11 -> x1, local copies, waits for them, and re-layouts: 4.45 us -> 1.72 us
    pallas_call x1, Pallas kernels: 25.8 us -> 25 us  [body(): pl.pallas_call(kernel, out_shape=jax.ShapeDtypeStruct(state.shape, f32),...]
where the time goes in v2:
time: 27 us; the launch traced here: 26.8 us
  Pallas kernels  25 us (93%)
  local copies, waits for them, and re-layouts  1.72 us (6%)
    pallas_call x1, Pallas kernels, body(): pl.pallas_call(kernel, out_shape=jax.ShapeDtypeStruct(state.shape, f32),...  25 us
    unnamed x1, local copies, waits for them, and re-layouts  1.72 us

profile of v2, /device:TPU:3, one launch (start us, length us, event | category | flops | bytes accessed | tf_op | source)
XLA Modules:
  0.0 26.8 jit_solution(16338669195899755733)
XLA Ops:
  0.0 25.0 %shard_map.55 = f32[1,20,2,16,128]{4,3,2,1,0:T(8,128)} custom-call(f32[1,20,2,16,128]{4,3,2,1,0:T(8,128)} %state_hbm.1, s32[4,2,16]{2,1,0:T(2,128)} %levels_hbm.1, f32[2,2,16,128]{3,2,1,0:T(8,128)} %flux_hbm.1, s32[19]{0:T(128)} %prey_hbm.1, f32[19]{0:T(128)} %rate_hbm.1), custom_call_target="tpu_custom_call" | custom-call | tf_op jit(solution)/shard_map/pallas_call | solution.py:349
  25.1 1.7 %copy.7 = f32[1,20,2,16,128]{4,3,2,1,0:T(8,128)} copy(f32[1,20,2,16,128]{4,3,2,1,0:T(8,128)} %shard_map.55) | data formatting | bytes 655360

commit v3 on v2

--- a/solution.py
+++ b/solution.py
@@ -19,9 +19,9 @@
 
 
 def kernel(
-    state_hbm, levels_hbm, flux_hbm, prey_hbm, rate_hbm, out_hbm,
+    state_hbm, levels_hbm, flux_hbm, prey_hbm, rate_hbm, out_ref,
     levels_ref, prey_ref, rate_ref, raw, cur, tanhs, hx, ys, yr, wet, flux, run, light, heat,
-    load_sem, small_sem, store_sem, send_sem, recv_sem, pair_send, pair_recv,
+    load_sem, small_sem, send_sem, recv_sem, pair_send, pair_recv, ready_sem,
 ):
     groups = cur.shape[1]
     size_x, size_y, depth = cur.shape[3:]
@@ -38,11 +38,6 @@
     def load(g):
         return pltpu.make_async_copy(state_hbm.at[0, pl.ds(4 * g, 4)], raw.at[g], load_sem.at[g])
 
-    def store(g):
-        return pltpu.make_async_copy(
-            cur.at[STEPS, g], out_hbm.at[0, pl.ds(4 * g, 4)], store_sem.at[g]
-        )
-
     levels_load = pltpu.make_async_copy(levels_hbm, levels_ref, small_sem.at[0])
     flux_load = pltpu.make_async_copy(flux_hbm, flux.at[0], small_sem.at[1])
     prey_load = pltpu.make_async_copy(prey_hbm, prey_ref, small_sem.at[2])
@@ -59,7 +54,10 @@
         @pl.when(has[side])
         def _():
             pl.semaphore_signal(barrier, inc=1, device_id=peer[side], device_id_type=MESH)
-    pl.semaphore_signal(barrier, inc=1, device_id=partner, device_id_type=MESH)
+
+    @pl.when(jnp.logical_not(is_ocean))
+    def _():
+        pl.semaphore_signal(barrier, inc=1, device_id=partner, device_id_type=MESH)
 
     for side in (WEST, EAST):
         @pl.when(jnp.logical_not(has[side]))
@@ -218,6 +216,7 @@
                         forcing = of_u * u + of_v * v + of_heat * heat[i] + ageing
                         new = wet[c, i] * (centre + DT * (NU * spread - advect + forcing))
                         put(s + 1, f, c, i, new)
+                        out_ref[0, 4 * f + c, i] = new
                         total = new if total is None else total + new
 
                     @pl.when(jnp.logical_and(f < 2, s < NSUB))
@@ -231,10 +230,6 @@
                 @pl.when(jnp.logical_and(s == NSUB - 1, f == 1))
                 def _():
                     pair_copy().start()
-
-                @pl.when(s == NSUB)
-                def _():
-                    store(f).start()
                 return inner
             return lax.fori_loop(0, groups, field, carry)
 
@@ -297,6 +292,7 @@
                         reaction = rate * centre * tanhs[now, prey, i] - mortality * centre
                         new = wet[c, i] * (centre + DT * (NU * spread - advect + reaction))
                         put(s + 1, g, c, i, new)
+                        out_ref[0, t, i] = new
                         tanhs[later, t, i] = jnp.tanh(new)
 
                 @pl.when(s < NSUB)
@@ -318,11 +314,8 @@
                             preferred_element_type=jnp.float32,
                         )
                         heat[i] = SURFACE * jnp.exp(-overhead) * (1.0 - jnp.exp(-attenuation))
+                    pl.semaphore_wait(ready_sem, 1)
                     pair_copy().start()
-
-                @pl.when(s == NSUB)
-                def _():
-                    store(g).start()
                 return inner
             return lax.fori_loop(0, groups, group, carry)
 
@@ -330,15 +323,17 @@
         wait_sends(False)
         pair_copy().wait_send()
 
-    greeted = 1
+    greeted = is_ocean.astype(jnp.int32)
     for side in range(4):
         greeted = greeted + has[side].astype(jnp.int32)
     pl.semaphore_wait(barrier, greeted)
 
+    @pl.when(is_ocean)
+    def _():
+        pl.semaphore_signal(ready_sem, inc=1, device_id=partner, device_id_type=MESH)
+
     pl.when(is_ocean)(ocean_part)
     pl.when(jnp.logical_not(is_ocean))(tracer_part)
-    for g in range(groups):
-        store(g).wait()
 
 
 def body(state, levels, old_flux, eco_prey, eco_rate):
@@ -348,9 +343,9 @@
     tile = (size_x, size_y, depth)
     return pl.pallas_call(
         kernel,
-        out_shape=jax.ShapeDtypeStruct(state.shape, f32),
-        in_specs=[pl.BlockSpec(memory_space=pl.ANY)] * 5,
-        out_specs=pl.BlockSpec(memory_space=pl.ANY),
+        out_shape=pltpu.VMEM(state.shape, f32),
+        in_specs=[pl.BlockSpec(memory_space=pltpu.HBM)] * 5,
+        out_specs=pl.BlockSpec(memory_space=pltpu.VMEM),
         scratch_shapes=[
             pltpu.VMEM(levels.shape, levels.dtype),
             pltpu.SMEM(eco_prey.shape, eco_prey.dtype),
@@ -368,11 +363,11 @@
             pltpu.VMEM(tile, f32),
             pltpu.SemaphoreType.DMA((groups,)),
             pltpu.SemaphoreType.DMA((4,)),
-            pltpu.SemaphoreType.DMA((groups,)),
             pltpu.SemaphoreType.DMA((STEPS, groups, 4)),
             pltpu.SemaphoreType.DMA((STEPS, groups, 4)),
             pltpu.SemaphoreType.DMA,
             pltpu.SemaphoreType.DMA,
+            pltpu.SemaphoreType.REGULAR,
         ],
         compiler_params=pltpu.CompilerParams(
             collective_id=0, has_side_effects=True, vmem_limit_bytes=60 * 1024 * 1024

time: 27 us -> 25.6 us (0.948)
  local copies, waits for them, and re-layouts: 1.72 us -> 0.73 us
  Pallas kernels: 25 us -> 24.7 us
    unnamed x1, local copies, waits for them, and re-layouts: 1.72 us -> 0.73 us
    pallas_call x1, Pallas kernels: 25 us -> 24.7 us  [body(): pl.pallas_call(kernel, out_shape=pltpu.VMEM(state.shape, f32), in_specs=[...]
where the time goes in v3:
time: 25.6 us; the launch traced here: 25.4 us
  Pallas kernels  24.7 us (96%)
  local copies, waits for them, and re-layouts  0.73 us (3%)
    pallas_call x1, Pallas kernels, body(): pl.pallas_call(kernel, out_shape=pltpu.VMEM(state.shape, f32), in_specs=[...  24.7 us
    unnamed x1, local copies, waits for them, and re-layouts  0.73 us

profile of v3, /device:TPU:3, one launch (start us, length us, event | category | flops | bytes accessed | tf_op | source)
XLA Modules:
  0.0 25.4 jit_solution(16580228821578567245)
XLA Ops:
  0.0 24.7 %shard_map.55 = f32[1,20,2,16,128]{4,3,2,1,0:T(8,128)S(1)} custom-call(f32[1,20,2,16,128]{4,3,2,1,0:T(8,128)} %state_hbm.1, s32[4,2,16]{2,1,0:T(2,128)} %levels_hbm.1, f32[2,2,16,128]{3,2,1,0:T(8,128)} %flux_hbm.1, s32[19]{0:T(128)} %prey_hbm.1, f32[19]{0:T(128)} %rate_hbm.1), custom_call_target="tpu_custom_call" | custom-call | tf_op jit(solution)/shard_map/pallas_call | solution.py:344
  24.7 0.7 %copy.7 = f32[1,20,2,16,128]{4,3,2,1,0:T(8,128)} copy(f32[1,20,2,16,128]{4,3,2,1,0:T(8,128)S(1)} %shard_map.55) | data formatting | bytes 655360

commit v4 on v3

--- a/solution.py
+++ b/solution.py
@@ -144,10 +144,13 @@
             return lax.fori_loop(0, groups, group, carry)
         lax.fori_loop(0, STEPS, step, 0)
 
-    def put(s, g, c, i, value):
-        cur[s, g, c, i] = value
-        ys[s, 0, g, pl.ds(c * size_x + i, 1), :] = value[0:1]
-        ys[s, 1, g, pl.ds(c * size_x + i, 1), :] = value[last_y:]
+    tiles = [(c, i) for c in range(4) for i in range(size_x)]
+
+    def put(s, g, values):
+        for (c, i), value in zip(tiles, values):
+            cur[s, g, c, i] = value
+            ys[s, 0, g, pl.ds(c * size_x + i, 1), :] = value[0:1]
+            ys[s, 1, g, pl.ds(c * size_x + i, 1), :] = value[last_y:]
 
     def north_of(value, s, g, c, i):
         arrived = yr[s, 1, g, pl.ds(c * size_x + i, 1), :]
@@ -160,9 +163,7 @@
     def ocean_part():
         def first(g, carry):
             load(g).wait()
-            for c in range(4):
-                for i in range(size_x):
-                    put(0, g, c, i, raw[g, c, i] * wet[c, i])
+            put(0, g, [raw[g, c, i] * wet[c, i] for c, i in tiles])
             start_copies(0, g, True)
             return carry
 
@@ -192,40 +193,43 @@
                 of_v = jnp.where(f == 0, CORIOLIS, jnp.where(f == 1, -DRAG, 0.0))
                 of_heat = jnp.where(f == 2, 1.0, 0.0)
                 ageing = jnp.where(f == 4, 1.0, 0.0)
-                for i in range(size_x):
-                    total = None
-                    for c in range(4):
-                        a, b = c // 2, c % 2
-                        centre = cur[s, f, c, i]
-                        if a == 0:
-                            to_east = cur[s, f, 2 + b, i]
-                            to_west = cur[s, f, 2 + b, i - 1] if i > 0 else hx[s, WEST, f, b]
-                        else:
-                            to_west = cur[s, f, b, i]
-                            to_east = cur[s, f, b, i + 1] if i < last_x else hx[s, EAST, f, b]
-                        other = cur[s, f, 2 * a + 1 - b, i]
-                        if b == 0:
-                            to_north = other
-                            to_south = south_of(other, s, f, c + 1, i)
-                        else:
-                            to_south = other
-                            to_north = north_of(other, s, f, c - 1, i)
-                        u, v = cur[s, 0, c, i], cur[s, 1, c, i]
-                        spread = to_east + to_west + to_north + to_south - 4.0 * centre
-                        advect = u * (to_east - to_west) * 0.5 + v * (to_north - to_south) * 0.5
-                        forcing = of_u * u + of_v * v + of_heat * heat[i] + ageing
-                        new = wet[c, i] * (centre + DT * (NU * spread - advect + forcing))
-                        put(s + 1, f, c, i, new)
-                        out_ref[0, 4 * f + c, i] = new
-                        total = new if total is None else total + new
-
-                    @pl.when(jnp.logical_and(f < 2, s < NSUB))
-                    def _():
+                values = []
+                for c, i in tiles:
+                    a, b = c // 2, c % 2
+                    centre = cur[s, f, c, i]
+                    if a == 0:
+                        to_east = cur[s, f, 2 + b, i]
+                        to_west = cur[s, f, 2 + b, i - 1] if i > 0 else hx[s, WEST, f, b]
+                    else:
+                        to_west = cur[s, f, b, i]
+                        to_east = cur[s, f, b, i + 1] if i < last_x else hx[s, EAST, f, b]
+                    other = cur[s, f, 2 * a + 1 - b, i]
+                    if b == 0:
+                        to_north = other
+                        to_south = south_of(other, s, f, c + 1, i)
+                    else:
+                        to_south = other
+                        to_north = north_of(other, s, f, c - 1, i)
+                    u, v = cur[s, 0, c, i], cur[s, 1, c, i]
+                    spread = to_east + to_west + to_north + to_south - 4.0 * centre
+                    advect = u * (to_east - to_west) * 0.5 + v * (to_north - to_south) * 0.5
+                    forcing = of_u * u + of_v * v + of_heat * heat[i] + ageing
+                    values.append(wet[c, i] * (centre + DT * (NU * spread - advect + forcing)))
+
+                put(s + 1, f, values)
+
+                @pl.when(s < NSUB)
+                def _():
+                    start_copies(s + 1, f, True)
+
+                for (c, i), value in zip(tiles, values):
+                    out_ref[0, 4 * f + c, i] = value
+
+                @pl.when(jnp.logical_and(f < 2, s < NSUB))
+                def _():
+                    for i in range(size_x):
+                        total = sum(value for (_, row), value in zip(tiles, values) if row == i)
                         run[f, i] = run[f, i] + total * (0.25 / NSUB)
-
-                @pl.when(s < NSUB)
-                def _():
-                    start_copies(s + 1, f, True)
 
                 @pl.when(jnp.logical_and(s == NSUB - 1, f == 1))
                 def _():
@@ -240,12 +244,11 @@
     def tracer_part():
         def first(g, carry):
             load(g).wait()
-            for c in range(4):
-                for i in range(size_x):
-                    value = raw[g, c, i] * wet[c, i]
-                    put(0, g, c, i, value)
-                    tanhs[0, 4 * g + c, i] = jnp.tanh(value)
+            values = [raw[g, c, i] * wet[c, i] for c, i in tiles]
+            put(0, g, values)
             start_copies(0, g, False)
+            for (c, i), value in zip(tiles, values):
+                tanhs[0, 4 * g + c, i] = jnp.tanh(value)
             return carry
 
         lax.fori_loop(0, groups, first, 0)
@@ -271,6 +274,7 @@
 
             def group(g, inner):
                 wait_arrivals(s, g, False)
+                values = []
                 for c in range(4):
                     t = 4 * g + c
                     living = jnp.where(t < species, 1.0, 0.0)
@@ -290,14 +294,18 @@
                             + flux[which, 1, i] * (to_north - to_south) * 0.5
                         )
                         reaction = rate * centre * tanhs[now, prey, i] - mortality * centre
-                        new = wet[c, i] * (centre + DT * (NU * spread - advect + reaction))
-                        put(s + 1, g, c, i, new)
-                        out_ref[0, t, i] = new
-                        tanhs[later, t, i] = jnp.tanh(new)
+                        values.append(
+                            wet[c, i] * (centre + DT * (NU * spread - advect + reaction))
+                        )
+                put(s + 1, g, values)
 
                 @pl.when(s < NSUB)
                 def _():
                     start_copies(s + 1, g, False)
+
+                for (c, i), value in zip(tiles, values):
+                    out_ref[0, 4 * g + c, i] = value
+                    tanhs[later, 4 * g + c, i] = jnp.tanh(value)
 
                 @pl.when(jnp.logical_and(s == NSUB - 1, g == 0))
                 def _():

time: 25.6 us -> 25.4 us (level)
  no operation moved by 1% of the time
where the time goes in v4:
time: 25.4 us; the launch traced here: 25.3 us
  Pallas kernels  24.6 us (97%)
  local copies, waits for them, and re-layouts  0.73 us (3%)
    pallas_call x1, Pallas kernels, body(): pl.pallas_call(kernel, out_shape=pltpu.VMEM(state.shape, f32), in_specs=[...  24.6 us
    unnamed x1, local copies, waits for them, and re-layouts  0.73 us

profile of v4, /device:TPU:3, one launch (start us, length us, event | category | flops | bytes accessed | tf_op | source)
XLA Modules:
  0.0 25.3 jit_solution(3910131110750226514)
XLA Ops:
  0.0 24.6 %shard_map.55 = f32[1,20,2,16,128]{4,3,2,1,0:T(8,128)S(1)} custom-call(f32[1,20,2,16,128]{4,3,2,1,0:T(8,128)} %state_hbm.1, s32[4,2,16]{2,1,0:T(2,128)} %levels_hbm.1, f32[2,2,16,128]{3,2,1,0:T(8,128)} %flux_hbm.1, s32[19]{0:T(128)} %prey_hbm.1, f32[19]{0:T(128)} %rate_hbm.1), custom_call_target="tpu_custom_call" | custom-call | tf_op jit(solution)/shard_map/pallas_call | solution.py:352
  24.6 0.7 %copy.7 = f32[1,20,2,16,128]{4,3,2,1,0:T(8,128)} copy(f32[1,20,2,16,128]{4,3,2,1,0:T(8,128)S(1)} %shard_map.55) | data formatting | bytes 655360

commit v5 on v4

--- a/solution.py
+++ b/solution.py
@@ -20,10 +20,12 @@
 
 def kernel(
     state_hbm, levels_hbm, flux_hbm, prey_hbm, rate_hbm, out_ref,
-    levels_ref, prey_ref, rate_ref, raw, cur, tanhs, hx, ys, yr, wet, flux, run, light, heat,
+    levels_ref, prey_ref, rate_ref, raw, cur, tanhs, preys, hosts, hx, ys, yr, wet, wetc, flux, run, light, heat,
     load_sem, small_sem, send_sem, recv_sem, pair_send, pair_recv, ready_sem,
 ):
-    groups = cur.shape[1]
+    groups = raw.shape[0]
+    guest = groups - 1
+    own = guest
     size_x, size_y, depth = cur.shape[3:]
     last_x, last_y = size_x - 1, size_y - 1
     species = prey_ref.shape[0]
@@ -84,8 +86,8 @@
             active.append(jnp.sum(spread, axis=1, keepdims=True))
         most = jnp.maximum(jnp.maximum(active[0], active[1]), jnp.maximum(active[2], active[3]))
         for c in range(4):
-            mine = jnp.where(is_ocean, active[c], most)
-            wet[c, i] = jnp.where(level_k < mine, 1.0, 0.0)
+            wet[c, i] = jnp.where(level_k < active[c], 1.0, 0.0)
+        wetc[i] = jnp.where(level_k < most, 1.0, 0.0)
 
     run[...] = jnp.zeros(run.shape, jnp.float32)
     heat[...] = jnp.zeros(heat.shape, jnp.float32)
@@ -133,7 +135,30 @@
                     device_id=peer[side], device_id_type=MESH,
                 ).wait_recv()
 
-    def wait_sends(ocean):
+    def pair_copy(src, dst, n):
+        return pltpu.make_async_remote_copy(
+            src, dst, pair_send.at[n], pair_recv.at[n], device_id=partner, device_id_type=MESH
+        )
+
+    def flux_copy():
+        return pair_copy(run, flux.at[1], 0)
+
+    def light_copy():
+        return pair_copy(heat, light, 0)
+
+    def guest_copy():
+        return pair_copy(cur.at[0, guest], cur.at[0, groups], 1)
+
+    def result_copy():
+        return pair_copy(cur.at[STEPS, groups], out_ref.at[0, pl.ds(4 * guest, 4)], 1)
+
+    def prey_copy(s):
+        return pair_copy(preys.at[s], preys.at[s], 2 + s)
+
+    def host_copy(s):
+        return pair_copy(hosts.at[s], hosts.at[s], 2 + s)
+
+    def wait_sends(first, end, ocean):
         def step(s, carry):
             def group(g, inner):
                 for side in range(4):
@@ -141,7 +166,7 @@
                     def _():
                         copy_of(s, g, side, ocean).wait_send()
                 return inner
-            return lax.fori_loop(0, groups, group, carry)
+            return lax.fori_loop(first, end, group, carry)
         lax.fori_loop(0, STEPS, step, 0)
 
     tiles = [(c, i) for c in range(4) for i in range(size_x)]
@@ -149,6 +174,10 @@
     def put(s, g, values):
         for (c, i), value in zip(tiles, values):
             cur[s, g, c, i] = value
+        put_rows(s, g, values)
+
+    def put_rows(s, g, values):
+        for (c, i), value in zip(tiles, values):
             ys[s, 0, g, pl.ds(c * size_x + i, 1), :] = value[0:1]
             ys[s, 1, g, pl.ds(c * size_x + i, 1), :] = value[last_y:]
 
@@ -159,6 +188,30 @@
     def south_of(value, s, g, c, i):
         arrived = yr[s, 0, g, pl.ds(c * size_x + i, 1), :]
         return jnp.where(rows == 0, arrived, pltpu.roll(value, 1, 0))
+
+    def tracer_values(s, which, g, start, prey_tile):
+        values = []
+        for c in range(4):
+            t = start + c
+            living = jnp.where(t < species, 1.0, 0.0)
+            slot = jnp.minimum(t, species - 1)
+            rate = rate_ref[slot] * living
+            mortality = MORTALITY * living
+            prey = prey_ref[slot]
+            for i in range(size_x):
+                centre = cur[s, g, c, i]
+                to_west = cur[s, g, c, i - 1] if i > 0 else hx[s, WEST, g, c]
+                to_east = cur[s, g, c, i + 1] if i < last_x else hx[s, EAST, g, c]
+                to_north = north_of(centre, s, g, c, i)
+                to_south = south_of(centre, s, g, c, i)
+                spread = to_east + to_west + to_north + to_south - 4.0 * centre
+                advect = (
+                    flux[which, 0, i] * (to_east - to_west) * 0.5
+                    + flux[which, 1, i] * (to_north - to_south) * 0.5
+                )
+                reaction = rate * centre * prey_tile(prey, c, i) - mortality * centre
+                values.append(wetc[i] * (centre + DT * (NU * spread - advect + reaction)))
+        return values
 
     def ocean_part():
         def first(g, carry):
@@ -172,10 +225,12 @@
         prey_load.wait()
         rate_load.wait()
 
-        def pair_copy():
-            return pltpu.make_async_remote_copy(
-                run, flux.at[1], pair_send, pair_recv, device_id=partner, device_id_type=MESH
-            )
+        guest_copy().wait_recv()
+        values = [cur[0, groups, c, i] for c, i in tiles]
+        put_rows(0, groups, values)
+        start_copies(0, groups, False)
+        for (c, i), value in zip(tiles, values):
+            hosts[0, c, i] = jnp.tanh(value)
 
         def step(s, carry):
             def field(f, inner):
@@ -183,10 +238,7 @@
 
                 @pl.when(jnp.logical_and(s == NSUB, f == 2))
                 def _():
-                    pltpu.make_async_remote_copy(
-                        light, light, pair_send, pair_recv,
-                        device_id=partner, device_id_type=MESH,
-                    ).wait_recv()
+                    light_copy().wait_recv()
                     heat[...] = light[...] * HEATING
 
                 of_u = jnp.where(f == 0, -DRAG, jnp.where(f == 1, -CORIOLIS, 0.0))
@@ -233,20 +285,57 @@
 
                 @pl.when(jnp.logical_and(s == NSUB - 1, f == 1))
                 def _():
-                    pair_copy().start()
+                    flux_copy().start()
+                    flux[1] = run[...]
+
                 return inner
-            return lax.fori_loop(0, groups, field, carry)
+            lax.fori_loop(0, groups, field, 0)
+
+            wait_arrivals(s, groups, False)
+            prey_copy(s).wait_recv()
+
+            def prey_tile(prey, c, i):
+                tile = preys[s, c, i]
+                for h in range(4):
+                    tile = jnp.where(prey == 4 * guest + h, hosts[s, h, i], tile)
+                return tile
+
+            values = tracer_values(s, s // NSUB, groups, 4 * guest, prey_tile)
+            put(s + 1, groups, values)
+
+            @pl.when(s < NSUB)
+            def _():
+                start_copies(s + 1, groups, False)
+                for (c, i), value in zip(tiles, values):
+                    hosts[s + 1, c, i] = jnp.tanh(value)
+                host_copy(s + 1).start()
+
+            return carry
 
         lax.fori_loop(0, STEPS, step, 0)
-        wait_sends(True)
-        pair_copy().wait_send()
+        result_copy().start()
+        wait_sends(0, groups, True)
+        wait_sends(groups, groups + 1, False)
+        flux_copy().wait_send()
+        for s in range(1, STEPS):
+            host_copy(s).wait_send()
+        result_copy().wait_send()
 
     def tracer_part():
         def first(g, carry):
             load(g).wait()
-            values = [raw[g, c, i] * wet[c, i] for c, i in tiles]
+            values = [raw[g, c, i] * wetc[i] for c, i in tiles]
             put(0, g, values)
-            start_copies(0, g, False)
+
+            @pl.when(g < own)
+            def _():
+                start_copies(0, g, False)
+
+            @pl.when(g == guest)
+            def _():
+                pl.semaphore_wait(ready_sem, 1)
+                guest_copy().start()
+
             for (c, i), value in zip(tiles, values):
                 tanhs[0, 4 * g + c, i] = jnp.tanh(value)
             return carry
@@ -256,47 +345,33 @@
         prey_load.wait()
         rate_load.wait()
 
-        def pair_copy():
-            return pltpu.make_async_remote_copy(
-                heat, light, pair_send, pair_recv, device_id=partner, device_id_type=MESH
-            )
+        def send_preys(s):
+            for c in range(4):
+                prey = prey_ref[min(4 * guest + c, species - 1)]
+                for i in range(size_x):
+                    preys[s, c, i] = tanhs[lax.rem(s, 2), prey, i]
+            prey_copy(s).start()
+
+        send_preys(0)
 
         def step(s, carry):
             now, later = lax.rem(s, 2), lax.rem(s + 1, 2)
-            which = s // NSUB
+
+            @pl.when(s > 0)
+            def _():
+                host_copy(s).wait_recv()
+                for c, i in tiles:
+                    tanhs[now, 4 * guest + c, i] = hosts[s, c, i]
 
             @pl.when(s == NSUB)
             def _():
-                pltpu.make_async_remote_copy(
-                    flux.at[1], flux.at[1], pair_send, pair_recv,
-                    device_id=partner, device_id_type=MESH,
-                ).wait_recv()
+                flux_copy().wait_recv()
 
             def group(g, inner):
                 wait_arrivals(s, g, False)
-                values = []
-                for c in range(4):
-                    t = 4 * g + c
-                    living = jnp.where(t < species, 1.0, 0.0)
-                    slot = jnp.minimum(t, species - 1)
-                    rate = rate_ref[slot] * living
-                    mortality = MORTALITY * living
-                    prey = prey_ref[slot]
-                    for i in range(size_x):
-                        centre = cur[s, g, c, i]
-                        to_west = cur[s, g, c, i - 1] if i > 0 else hx[s, WEST, g, c]
-                        to_east = cur[s, g, c, i + 1] if i < last_x else hx[s, EAST, g, c]
-                        to_north = north_of(centre, s, g, c, i)
-                        to_south = south_of(centre, s, g, c, i)
-                        spread = to_east + to_west + to_north + to_south - 4.0 * centre
-                        advect = (
-                            flux[which, 0, i] * (to_east - to_west) * 0.5
-                            + flux[which, 1, i] * (to_north - to_south) * 0.5
-                        )
-                        reaction = rate * centre * tanhs[now, prey, i] - mortality * centre
-                        values.append(
-                            wet[c, i] * (centre + DT * (NU * spread - advect + reaction))
-                        )
+                values = tracer_values(
+                    s, s // NSUB, g, 4 * g, lambda prey, c, i: tanhs[now, prey, i]
+                )
                 put(s + 1, g, values)
 
                 @pl.when(s < NSUB)
@@ -316,20 +391,30 @@
                     for i in range(size_x):
                         green = cur[s + 1, 0, 0, i]
                         soft = jnp.maximum(green, 0.0) + jnp.log(1.0 + jnp.exp(-jnp.abs(green)))
-                        attenuation = wet[0, i] * (0.03 + 0.05 * soft)
+                        attenuation = wetc[i] * (0.03 + 0.05 * soft)
                         overhead = jnp.dot(
                             attenuation, above, precision=lax.Precision.HIGHEST,
                             preferred_element_type=jnp.float32,
                         )
                         heat[i] = SURFACE * jnp.exp(-overhead) * (1.0 - jnp.exp(-attenuation))
-                    pl.semaphore_wait(ready_sem, 1)
-                    pair_copy().start()
+                    light_copy().start()
+
                 return inner
-            return lax.fori_loop(0, groups, group, carry)
+            lax.fori_loop(0, own, group, 0)
+
+            @pl.when(s < NSUB)
+            def _():
+                send_preys(s + 1)
+
+            return carry
 
         lax.fori_loop(0, STEPS, step, 0)
-        wait_sends(False)
-        pair_copy().wait_send()
+        wait_sends(0, own, False)
+        guest_copy().wait_send()
+        light_copy().wait_send()
+        for s in range(STEPS):
+            prey_copy(s).wait_send()
+        result_copy().wait_recv()
 
     greeted = is_ocean.astype(jnp.int32)
     for side in range(4):
@@ -347,6 +432,7 @@
 def body(state, levels, old_flux, eco_prey, eco_rate):
     channels, size_x, size_y, depth = state.shape[1:]
     groups = channels // 4
+    slots = groups + 1
     f32 = jnp.float32
     tile = (size_x, size_y, depth)
     return pl.pallas_call(
@@ -359,22 +445,25 @@
             pltpu.SMEM(eco_prey.shape, eco_prey.dtype),
             pltpu.SMEM(eco_rate.shape, eco_rate.dtype),
             pltpu.VMEM((groups, 4) + tile, f32),
-            pltpu.VMEM((STEPS + 1, groups, 4) + tile, f32),
+            pltpu.VMEM((STEPS + 1, slots, 4) + tile, f32),
             pltpu.VMEM((2, channels) + tile, f32),
-            pltpu.VMEM((STEPS, 2, groups, 4, size_y, depth), f32),
-            pltpu.VMEM((STEPS + 1, 2, groups, 4 * size_x, depth), f32),
-            pltpu.VMEM((STEPS, 2, groups, 4 * size_x, depth), f32),
+            pltpu.VMEM((STEPS, 4) + tile, f32),
+            pltpu.VMEM((STEPS, 4) + tile, f32),
+            pltpu.VMEM((STEPS, 2, slots, 4, size_y, depth), f32),
+            pltpu.VMEM((STEPS + 1, 2, slots, 4 * size_x, depth), f32),
+            pltpu.VMEM((STEPS, 2, slots, 4 * size_x, depth), f32),
             pltpu.VMEM((4,) + tile, f32),
+            pltpu.VMEM(tile, f32),
             pltpu.VMEM((2, 2) + tile, f32),
             pltpu.VMEM((2,) + tile, f32),
             pltpu.VMEM(tile, f32),
             pltpu.VMEM(tile, f32),
             pltpu.SemaphoreType.DMA((groups,)),
             pltpu.SemaphoreType.DMA((4,)),
-            pltpu.SemaphoreType.DMA((STEPS, groups, 4)),
-            pltpu.SemaphoreType.DMA((STEPS, groups, 4)),
-            pltpu.SemaphoreType.DMA,
-            pltpu.SemaphoreType.DMA,
+            pltpu.SemaphoreType.DMA((STEPS, slots, 4)),
+            pltpu.SemaphoreType.DMA((STEPS, slots, 4)),
+            pltpu.SemaphoreType.DMA((2 + STEPS,)),
+            pltpu.SemaphoreType.DMA((2 + STEPS,)),
             pltpu.SemaphoreType.REGULAR,
         ],
         compiler_params=pltpu.CompilerParams(

time: 25.4 us -> 31.7 us (1.25)
  the two profiles are of different devices: /device:TPU:3 before, /device:TPU:0 now
where the time goes in v5:
time: 31.7 us; the launch traced here: 31.6 us
  Pallas kernels  30.8 us (97%)
  local copies, waits for them, and re-layouts  0.73 us (2%)
    pallas_call x1, Pallas kernels, body(): pl.pallas_call(kernel, out_shape=pltpu.VMEM(state.shape, f32), in_specs=[...  30.8 us
    unnamed x1, local copies, waits for them, and re-layouts  0.73 us

profile of v5, /device:TPU:0, one launch (start us, length us, event | category | flops | bytes accessed | tf_op | source)
XLA Modules:
  0.0 31.6 jit_solution(15416476917007207489)
XLA Ops:
  0.0 30.8 %shard_map.55 = f32[1,20,2,16,128]{4,3,2,1,0:T(8,128)S(1)} custom-call(f32[1,20,2,16,128]{4,3,2,1,0:T(8,128)} %state_hbm.1, s32[4,2,16]{2,1,0:T(2,128)} %levels_hbm.1, f32[2,2,16,128]{3,2,1,0:T(8,128)} %flux_hbm.1, s32[19]{0:T(128)} %prey_hbm.1, f32[19]{0:T(128)} %rate_hbm.1), custom_call_target="tpu_custom_call" | custom-call | tf_op jit(solution)/shard_map/pallas_call | solution.py:438
  30.9 0.7 %copy.7 = f32[1,20,2,16,128]{4,3,2,1,0:T(8,128)} copy(f32[1,20,2,16,128]{4,3,2,1,0:T(8,128)S(1)} %shard_map.55) | data formatting | bytes 655360

commit v6 on v4

--- a/solution.py
+++ b/solution.py
@@ -16,6 +16,7 @@
 SURFACE = 8.0
 MESH = pl.DeviceIdType.MESH
 WEST, EAST, SOUTH, NORTH = 0, 1, 2, 3
+BATCHES = 2
 
 
 def kernel(
@@ -32,8 +33,10 @@
     nx, ny = lax.axis_size("gx"), lax.axis_size("gy")
     is_ocean = half == 0
     has = (gx > 0, gx < nx - 1, gy > 0, gy < ny - 1)
-    peer = ({"gx": gx - 1}, {"gx": gx + 1}, {"gy": gy - 1}, {"gy": gy + 1})
-    partner = {"half": 1 - half}
+    peer = ((half, gx - 1, gy), (half, gx + 1, gy), (half, gx, gy - 1), (half, gx, gy + 1))
+    partner = (1 - half, gx, gy)
+    bounds = [groups * n // BATCHES for n in range(BATCHES + 1)]
+    batches = [(n, bounds[n], bounds[n + 1]) for n in range(BATCHES)]
 
     def load(g):
         return pltpu.make_async_copy(state_hbm.at[0, pl.ds(4 * g, 4)], raw.at[g], load_sem.at[g])
@@ -90,59 +93,60 @@
     run[...] = jnp.zeros(run.shape, jnp.float32)
     heat[...] = jnp.zeros(heat.shape, jnp.float32)
 
-    def x_copy(s, g, side, ocean):
-        row = 0 if side == WEST else last_x
-        if ocean:
-            channels = pl.ds(0, 2) if side == WEST else pl.ds(2, 2)
-            src = cur.at[s, g, channels, row]
-            dst = hx.at[s, 1 - side, g, pl.ds(0, 2)]
+    def copy_of(s, batch, side, ocean):
+        n, low, high = batch
+        span = pl.ds(low, high - low)
+        if side < 2:
+            row = 0 if side == WEST else last_x
+            if ocean:
+                channels = pl.ds(0, 2) if side == WEST else pl.ds(2, 2)
+                src = cur.at[s, span, channels, row]
+                dst = hx.at[s, 1 - side, span, pl.ds(0, 2)]
+            else:
+                src = cur.at[s, span, :, row]
+                dst = hx.at[s, 1 - side, span]
         else:
-            src = cur.at[s, g, :, row]
-            dst = hx.at[s, 1 - side, g]
+            src = ys.at[s, side - 2, span]
+            dst = yr.at[s, 3 - side, span]
+        lands = 1 - side if side < 2 else 5 - side
         return pltpu.make_async_remote_copy(
-            src, dst, send_sem.at[s, g, side], recv_sem.at[s, g, 1 - side],
+            src, dst, send_sem.at[side], recv_sem.at[s, n, lands],
             device_id=peer[side], device_id_type=MESH,
         )
 
-    def y_copy(s, g, side):
-        return pltpu.make_async_remote_copy(
-            ys.at[s, side - 2, g], yr.at[s, 3 - side, g],
-            send_sem.at[s, g, side], recv_sem.at[s, g, 5 - side],
-            device_id=peer[side], device_id_type=MESH,
-        )
-
-    def copy_of(s, g, side, ocean):
-        return x_copy(s, g, side, ocean) if side < 2 else y_copy(s, g, side)
-
-    def start_copies(s, g, ocean):
+    def start_copies(s, batch, ocean):
         for side in range(4):
             @pl.when(has[side])
             def _():
-                copy_of(s, g, side, ocean).start()
-
-    def wait_arrivals(s, g, ocean):
+                copy_of(s, batch, side, ocean).start()
+
+    def wait_arrivals(s, batch, ocean):
+        n, low, high = batch
+        span = pl.ds(low, high - low)
         for side in range(4):
             @pl.when(has[side])
             def _():
                 if side < 2:
-                    lands = hx.at[s, side, g, pl.ds(0, 2)] if ocean else hx.at[s, side, g]
+                    lands = hx.at[s, side, span, pl.ds(0, 2)] if ocean else hx.at[s, side, span]
                 else:
-                    lands = yr.at[s, side - 2, g]
+                    lands = yr.at[s, side - 2, span]
                 pltpu.make_async_remote_copy(
-                    lands, lands, send_sem.at[s, g, side], recv_sem.at[s, g, side],
+                    lands, lands, send_sem.at[side], recv_sem.at[s, n, side],
                     device_id=peer[side], device_id_type=MESH,
                 ).wait_recv()
 
     def wait_sends(ocean):
-        def step(s, carry):
-            def group(g, inner):
-                for side in range(4):
-                    @pl.when(has[side])
-                    def _():
-                        copy_of(s, g, side, ocean).wait_send()
-                return inner
-            return lax.fori_loop(0, groups, group, carry)
-        lax.fori_loop(0, STEPS, step, 0)
+        for side in range(4):
+            @pl.when(has[side])
+            def _():
+                if side < 2:
+                    sent = hx.at[:, side, :, pl.ds(0, 2)] if ocean else hx.at[:, side]
+                else:
+                    sent = yr.at[:, side - 2]
+                pltpu.make_async_remote_copy(
+                    sent, sent, send_sem.at[side], recv_sem.at[0, 0, side],
+                    device_id=peer[side], device_id_type=MESH,
+                ).wait_send()
 
     tiles = [(c, i) for c in range(4) for i in range(size_x)]
 
@@ -164,10 +168,11 @@
         def first(g, carry):
             load(g).wait()
             put(0, g, [raw[g, c, i] * wet[c, i] for c, i in tiles])
-            start_copies(0, g, True)
             return carry
 
-        lax.fori_loop(0, groups, first, 0)
+        for batch in batches:
+            lax.fori_loop(batch[1], batch[2], first, 0)
+            start_copies(0, batch, True)
         flux_load.wait()
         prey_load.wait()
         rate_load.wait()
@@ -179,8 +184,6 @@
 
         def step(s, carry):
             def field(f, inner):
-                wait_arrivals(s, f, True)
-
                 @pl.when(jnp.logical_and(s == NSUB, f == 2))
                 def _():
                     pltpu.make_async_remote_copy(
@@ -218,10 +221,6 @@
 
                 put(s + 1, f, values)
 
-                @pl.when(s < NSUB)
-                def _():
-                    start_copies(s + 1, f, True)
-
                 for (c, i), value in zip(tiles, values):
                     out_ref[0, 4 * f + c, i] = value
 
@@ -235,7 +234,15 @@
                 def _():
                     pair_copy().start()
                 return inner
-            return lax.fori_loop(0, groups, field, carry)
+
+            for batch in batches:
+                wait_arrivals(s, batch, True)
+                lax.fori_loop(batch[1], batch[2], field, 0)
+
+                @pl.when(s < NSUB)
+                def _():
+                    start_copies(s + 1, batch, True)
+            return carry
 
         lax.fori_loop(0, STEPS, step, 0)
         wait_sends(True)
@@ -246,12 +253,13 @@
             load(g).wait()
             values = [raw[g, c, i] * wet[c, i] for c, i in tiles]
             put(0, g, values)
-            start_copies(0, g, False)
             for (c, i), value in zip(tiles, values):
                 tanhs[0, 4 * g + c, i] = jnp.tanh(value)
             return carry
 
-        lax.fori_loop(0, groups, first, 0)
+        for batch in batches:
+            lax.fori_loop(batch[1], batch[2], first, 0)
+            start_copies(0, batch, False)
         flux_load.wait()
         prey_load.wait()
         rate_load.wait()
@@ -273,7 +281,6 @@
                 ).wait_recv()
 
             def group(g, inner):
-                wait_arrivals(s, g, False)
                 values = []
                 for c in range(4):
                     t = 4 * g + c
@@ -299,10 +306,6 @@
                         )
                 put(s + 1, g, values)
 
-                @pl.when(s < NSUB)
-                def _():
-                    start_copies(s + 1, g, False)
-
                 for (c, i), value in zip(tiles, values):
                     out_ref[0, 4 * g + c, i] = value
                     tanhs[later, 4 * g + c, i] = jnp.tanh(value)
@@ -325,7 +328,15 @@
                     pl.semaphore_wait(ready_sem, 1)
                     pair_copy().start()
                 return inner
-            return lax.fori_loop(0, groups, group, carry)
+
+            for batch in batches:
+                wait_arrivals(s, batch, False)
+                lax.fori_loop(batch[1], batch[2], group, 0)
+
+                @pl.when(s < NSUB)
+                def _():
+                    start_copies(s + 1, batch, False)
+            return carry
 
         lax.fori_loop(0, STEPS, step, 0)
         wait_sends(False)
@@ -371,8 +382,8 @@
             pltpu.VMEM(tile, f32),
             pltpu.SemaphoreType.DMA((groups,)),
             pltpu.SemaphoreType.DMA((4,)),
-            pltpu.SemaphoreType.DMA((STEPS, groups, 4)),
-            pltpu.SemaphoreType.DMA((STEPS, groups, 4)),
+            pltpu.SemaphoreType.DMA((4,)),
+            pltpu.SemaphoreType.DMA((STEPS, BATCHES, 4)),
             pltpu.SemaphoreType.DMA,
             pltpu.SemaphoreType.DMA,
             pltpu.SemaphoreType.REGULAR,

time: 25.4 us -> 27.7 us (1.091)
  the two profiles are of different devices: /device:TPU:3 before, /device:TPU:2 now
where the time goes in v6:
time: 27.7 us; the launch traced here: 27.5 us
  Pallas kernels  26.8 us (97%)
  local copies, waits for them, and re-layouts  0.73 us (3%)
    pallas_call x1, Pallas kernels, body(): pl.pallas_call(kernel, out_shape=pltpu.VMEM(state.shape, f32), in_specs=[...  26.8 us
    unnamed x1, local copies, waits for them, and re-layouts  0.73 us

profile of v6, /device:TPU:2, one launch (start us, length us, event | category | flops | bytes accessed | tf_op | source)
XLA Modules:
  0.0 27.5 jit_solution(18038127819825372727)
XLA Ops:
  0.0 26.8 %shard_map.55 = f32[1,20,2,16,128]{4,3,2,1,0:T(8,128)S(1)} custom-call(f32[1,20,2,16,128]{4,3,2,1,0:T(8,128)} %state_hbm.1, s32[4,2,16]{2,1,0:T(2,128)} %levels_hbm.1, f32[2,2,16,128]{3,2,1,0:T(8,128)} %flux_hbm.1, s32[19]{0:T(128)} %prey_hbm.1, f32[19]{0:T(128)} %rate_hbm.1), custom_call_target="tpu_custom_call" | custom-call | tf_op jit(solution)/shard_map/pallas_call | solution.py:363
  26.8 0.7 %copy.7 = f32[1,20,2,16,128]{4,3,2,1,0:T(8,128)} copy(f32[1,20,2,16,128]{4,3,2,1,0:T(8,128)S(1)} %shard_map.55) | data formatting | bytes 655360

commit v7 on v4

--- a/solution.py
+++ b/solution.py
@@ -32,8 +32,9 @@
     nx, ny = lax.axis_size("gx"), lax.axis_size("gy")
     is_ocean = half == 0
     has = (gx > 0, gx < nx - 1, gy > 0, gy < ny - 1)
-    peer = ({"gx": gx - 1}, {"gx": gx + 1}, {"gy": gy - 1}, {"gy": gy + 1})
-    partner = {"half": 1 - half}
+    peer = ((half, gx - 1, gy), (half, gx + 1, gy), (half, gx, gy - 1), (half, gx, gy + 1))
+    partner = (1 - half, gx, gy)
+    even = lax.rem(gy, 2) == 0
 
     def load(g):
         return pltpu.make_async_copy(state_hbm.at[0, pl.ds(4 * g, 4)], raw.at[g], load_sem.at[g])
@@ -90,33 +91,30 @@
     run[...] = jnp.zeros(run.shape, jnp.float32)
     heat[...] = jnp.zeros(heat.shape, jnp.float32)
 
-    def x_copy(s, g, side, ocean):
-        row = 0 if side == WEST else last_x
-        if ocean:
-            channels = pl.ds(0, 2) if side == WEST else pl.ds(2, 2)
-            src = cur.at[s, g, channels, row]
-            dst = hx.at[s, 1 - side, g, pl.ds(0, 2)]
+    def copy_of(s, g, side, ocean):
+        if side < 2:
+            row = 0 if side == WEST else last_x
+            if ocean:
+                channels = pl.ds(0, 2) if side == WEST else pl.ds(2, 2)
+                src = cur.at[s, g, channels, row]
+                dst = hx.at[s, 1 - side, g, pl.ds(0, 2)]
+            else:
+                src = cur.at[s, g, :, row]
+                dst = hx.at[s, 1 - side, g]
         else:
-            src = cur.at[s, g, :, row]
-            dst = hx.at[s, 1 - side, g]
+            src = ys.at[s, side - 2, g]
+            dst = yr.at[s, 3 - side, g]
+        lands = 1 - side if side < 2 else 5 - side
         return pltpu.make_async_remote_copy(
-            src, dst, send_sem.at[s, g, side], recv_sem.at[s, g, 1 - side],
+            src, dst, send_sem.at[side], recv_sem.at[s, g, lands],
             device_id=peer[side], device_id_type=MESH,
         )
 
-    def y_copy(s, g, side):
-        return pltpu.make_async_remote_copy(
-            ys.at[s, side - 2, g], yr.at[s, 3 - side, g],
-            send_sem.at[s, g, side], recv_sem.at[s, g, 5 - side],
-            device_id=peer[side], device_id_type=MESH,
-        )
-
-    def copy_of(s, g, side, ocean):
-        return x_copy(s, g, side, ocean) if side < 2 else y_copy(s, g, side)
-
     def start_copies(s, g, ocean):
-        for side in range(4):
-            @pl.when(has[side])
+        for side, turn in (
+            (SOUTH, None), (NORTH, None), (WEST, even), (EAST, None), (WEST, jnp.logical_not(even)),
+        ):
+            @pl.when(has[side] if turn is None else jnp.logical_and(has[side], turn))
             def _():
                 copy_of(s, g, side, ocean).start()
 
@@ -129,20 +127,22 @@
                 else:
                     lands = yr.at[s, side - 2, g]
                 pltpu.make_async_remote_copy(
-                    lands, lands, send_sem.at[s, g, side], recv_sem.at[s, g, side],
+                    lands, lands, send_sem.at[side], recv_sem.at[s, g, side],
                     device_id=peer[side], device_id_type=MESH,
                 ).wait_recv()
 
     def wait_sends(ocean):
-        def step(s, carry):
-            def group(g, inner):
-                for side in range(4):
-                    @pl.when(has[side])
-                    def _():
-                        copy_of(s, g, side, ocean).wait_send()
-                return inner
-            return lax.fori_loop(0, groups, group, carry)
-        lax.fori_loop(0, STEPS, step, 0)
+        for side in range(4):
+            @pl.when(has[side])
+            def _():
+                if side < 2:
+                    sent = hx.at[:, side, :, pl.ds(0, 2)] if ocean else hx.at[:, side]
+                else:
+                    sent = yr.at[:, side - 2]
+                pltpu.make_async_remote_copy(
+                    sent, sent, send_sem.at[side], recv_sem.at[0, 0, side],
+                    device_id=peer[side], device_id_type=MESH,
+                ).wait_send()
 
     tiles = [(c, i) for c in range(4) for i in range(size_x)]
 
@@ -180,7 +180,6 @@
         def step(s, carry):
             def field(f, inner):
                 wait_arrivals(s, f, True)
-
                 @pl.when(jnp.logical_and(s == NSUB, f == 2))
                 def _():
                     pltpu.make_async_remote_copy(
@@ -371,7 +370,7 @@
             pltpu.VMEM(tile, f32),
             pltpu.SemaphoreType.DMA((groups,)),
             pltpu.SemaphoreType.DMA((4,)),
-            pltpu.SemaphoreType.DMA((STEPS, groups, 4)),
+            pltpu.SemaphoreType.DMA((4,)),
             pltpu.SemaphoreType.DMA((STEPS, groups, 4)),
             pltpu.SemaphoreType.DMA,
             pltpu.SemaphoreType.DMA,

time: 25.4 us -> 24.4 us (0.961)
  Pallas kernels: 24.6 us -> 23.5 us
    pallas_call x1, Pallas kernels: 24.6 us -> 23.5 us  [body(): pl.pallas_call(kernel, out_shape=pltpu.VMEM(state.shape, f32), in_specs=[...]
where the time goes in v7:
time: 24.4 us; the launch traced here: 24.2 us
  Pallas kernels  23.5 us (96%)
  local copies, waits for them, and re-layouts  0.73 us (3%)
    pallas_call x1, Pallas kernels, body(): pl.pallas_call(kernel, out_shape=pltpu.VMEM(state.shape, f32), in_specs=[...  23.5 us
    unnamed x1, local copies, waits for them, and re-layouts  0.73 us

profile of v7, /device:TPU:3, one launch (start us, length us, event | category | flops | bytes accessed | tf_op | source)
XLA Modules:
  0.0 24.2 jit_solution(405658158276064566)
XLA Ops:
  0.0 23.5 %shard_map.55 = f32[1,20,2,16,128]{4,3,2,1,0:T(8,128)S(1)} custom-call(f32[1,20,2,16,128]{4,3,2,1,0:T(8,128)} %state_hbm.1, s32[4,2,16]{2,1,0:T(2,128)} %levels_hbm.1, f32[2,2,16,128]{3,2,1,0:T(8,128)} %flux_hbm.1, s32[19]{0:T(128)} %prey_hbm.1, f32[19]{0:T(128)} %rate_hbm.1), custom_call_target="tpu_custom_call" | custom-call | tf_op jit(solution)/shard_map/pallas_call | solution.py:351
  23.5 0.7 %copy.7 = f32[1,20,2,16,128]{4,3,2,1,0:T(8,128)} copy(f32[1,20,2,16,128]{4,3,2,1,0:T(8,128)S(1)} %shard_map.55) | data formatting | bytes 655360

commit v8 on v7

--- a/solution.py
+++ b/solution.py
@@ -91,45 +91,53 @@
     run[...] = jnp.zeros(run.shape, jnp.float32)
     heat[...] = jnp.zeros(heat.shape, jnp.float32)
 
-    def copy_of(s, g, side, ocean):
+    def copy_of(s, g, side, ocean, part=0):
         if side < 2:
             row = 0 if side == WEST else last_x
             if ocean:
                 channels = pl.ds(0, 2) if side == WEST else pl.ds(2, 2)
-                src = cur.at[s, g, channels, row]
                 dst = hx.at[s, 1 - side, g, pl.ds(0, 2)]
             else:
-                src = cur.at[s, g, :, row]
-                dst = hx.at[s, 1 - side, g]
+                channels = pl.ds(2 * part, 2)
+                dst = hx.at[s, 1 - side, g, channels]
+            src = cur.at[s, g, channels, row]
+            lands = 2 * part + 1 - side
         else:
             src = ys.at[s, side - 2, g]
             dst = yr.at[s, 3 - side, g]
-        lands = 1 - side if side < 2 else 5 - side
+            lands = 4 + 3 - side
         return pltpu.make_async_remote_copy(
             src, dst, send_sem.at[side], recv_sem.at[s, g, lands],
             device_id=peer[side], device_id_type=MESH,
         )
 
-    def start_copies(s, g, ocean):
-        for side, turn in (
-            (SOUTH, None), (NORTH, None), (WEST, even), (EAST, None), (WEST, jnp.logical_not(even)),
-        ):
+    def start_y(s, g):
+        for side in (SOUTH, NORTH):
+            @pl.when(has[side])
+            def _():
+                copy_of(s, g, side, False).start()
+
+    def start_x(s, g, ocean, part=0):
+        for side, turn in ((WEST, even), (EAST, None), (WEST, jnp.logical_not(even))):
             @pl.when(has[side] if turn is None else jnp.logical_and(has[side], turn))
             def _():
-                copy_of(s, g, side, ocean).start()
-
-    def wait_arrivals(s, g, ocean):
-        for side in range(4):
-            @pl.when(has[side])
-            def _():
-                if side < 2:
-                    lands = hx.at[s, side, g, pl.ds(0, 2)] if ocean else hx.at[s, side, g]
-                else:
-                    lands = yr.at[s, side - 2, g]
-                pltpu.make_async_remote_copy(
-                    lands, lands, send_sem.at[side], recv_sem.at[s, g, side],
-                    device_id=peer[side], device_id_type=MESH,
-                ).wait_recv()
+                copy_of(s, g, side, ocean, part).start()
+
+    def arrival(lands, s, g, side, n):
+        @pl.when(has[side])
+        def _():
+            pltpu.make_async_remote_copy(
+                lands, lands, send_sem.at[side], recv_sem.at[s, g, n],
+                device_id=peer[side], device_id_type=MESH,
+            ).wait_recv()
+
+    def wait_y(s, g):
+        for side in (SOUTH, NORTH):
+            arrival(yr.at[s, side - 2, g], s, g, side, 2 + side)
+
+    def wait_x(s, g, part=0):
+        for side in (WEST, EAST):
+            arrival(hx.at[s, side, g, pl.ds(2 * part, 2)], s, g, side, 2 * part + side)
 
     def wait_sends(ocean):
         for side in range(4):
@@ -146,8 +154,10 @@
 
     tiles = [(c, i) for c in range(4) for i in range(size_x)]
 
-    def put(s, g, values):
-        for (c, i), value in zip(tiles, values):
+    parts = [[(c, i) for c, i in tiles if c // 2 == part] for part in range(2)]
+
+    def put(s, g, values, where=tiles):
+        for (c, i), value in zip(where, values):
             cur[s, g, c, i] = value
             ys[s, 0, g, pl.ds(c * size_x + i, 1), :] = value[0:1]
             ys[s, 1, g, pl.ds(c * size_x + i, 1), :] = value[last_y:]
@@ -164,7 +174,8 @@
         def first(g, carry):
             load(g).wait()
             put(0, g, [raw[g, c, i] * wet[c, i] for c, i in tiles])
-            start_copies(0, g, True)
+            start_y(0, g)
+            start_x(0, g, True)
             return carry
 
         lax.fori_loop(0, groups, first, 0)
@@ -179,7 +190,8 @@
 
         def step(s, carry):
             def field(f, inner):
-                wait_arrivals(s, f, True)
+                wait_y(s, f)
+                wait_x(s, f)
                 @pl.when(jnp.logical_and(s == NSUB, f == 2))
                 def _():
                     pltpu.make_async_remote_copy(
@@ -219,7 +231,8 @@
 
                 @pl.when(s < NSUB)
                 def _():
-                    start_copies(s + 1, f, True)
+                    start_y(s + 1, f)
+                    start_x(s + 1, f, True)
 
                 for (c, i), value in zip(tiles, values):
                     out_ref[0, 4 * f + c, i] = value
@@ -243,11 +256,13 @@
     def tracer_part():
         def first(g, carry):
             load(g).wait()
-            values = [raw[g, c, i] * wet[c, i] for c, i in tiles]
-            put(0, g, values)
-            start_copies(0, g, False)
-            for (c, i), value in zip(tiles, values):
-                tanhs[0, 4 * g + c, i] = jnp.tanh(value)
+            for part, where in enumerate(parts):
+                values = [raw[g, c, i] * wet[c, i] for c, i in where]
+                put(0, g, values, where)
+                start_x(0, g, False, part)
+                for (c, i), value in zip(where, values):
+                    tanhs[0, 4 * g + c, i] = jnp.tanh(value)
+            start_y(0, g)
             return carry
 
         lax.fori_loop(0, groups, first, 0)
@@ -272,16 +287,17 @@
                 ).wait_recv()
 
             def group(g, inner):
-                wait_arrivals(s, g, False)
-                values = []
-                for c in range(4):
-                    t = 4 * g + c
-                    living = jnp.where(t < species, 1.0, 0.0)
-                    slot = jnp.minimum(t, species - 1)
-                    rate = rate_ref[slot] * living
-                    mortality = MORTALITY * living
-                    prey = prey_ref[slot]
-                    for i in range(size_x):
+                wait_y(s, g)
+                for part, where in enumerate(parts):
+                    wait_x(s, g, part)
+                    values = []
+                    for c, i in where:
+                        t = 4 * g + c
+                        living = jnp.where(t < species, 1.0, 0.0)
+                        slot = jnp.minimum(t, species - 1)
+                        rate = rate_ref[slot] * living
+                        mortality = MORTALITY * living
+                        prey = prey_ref[slot]
                         centre = cur[s, g, c, i]
                         to_west = cur[s, g, c, i - 1] if i > 0 else hx[s, WEST, g, c]
                         to_east = cur[s, g, c, i + 1] if i < last_x else hx[s, EAST, g, c]
@@ -296,15 +312,19 @@
                         values.append(
                             wet[c, i] * (centre + DT * (NU * spread - advect + reaction))
                         )
-                put(s + 1, g, values)
+                    put(s + 1, g, values, where)
+
+                    @pl.when(s < NSUB)
+                    def _():
+                        start_x(s + 1, g, False, part)
+
+                    for (c, i), value in zip(where, values):
+                        out_ref[0, 4 * g + c, i] = value
+                        tanhs[later, 4 * g + c, i] = jnp.tanh(value)
 
                 @pl.when(s < NSUB)
                 def _():
-                    start_copies(s + 1, g, False)
-
-                for (c, i), value in zip(tiles, values):
-                    out_ref[0, 4 * g + c, i] = value
-                    tanhs[later, 4 * g + c, i] = jnp.tanh(value)
+                    start_y(s + 1, g)
 
                 @pl.when(jnp.logical_and(s == NSUB - 1, g == 0))
                 def _():
@@ -371,7 +391,7 @@
             pltpu.SemaphoreType.DMA((groups,)),
             pltpu.SemaphoreType.DMA((4,)),
             pltpu.SemaphoreType.DMA((4,)),
-            pltpu.SemaphoreType.DMA((STEPS, groups, 4)),
+            pltpu.SemaphoreType.DMA((STEPS, groups, 6)),
             pltpu.SemaphoreType.DMA,
             pltpu.SemaphoreType.DMA,
             pltpu.SemaphoreType.REGULAR,

time: 24.4 us -> 24.5 us (level)
  no operation moved by 1% of the time
where the time goes in v8:
time: 24.5 us; the launch traced here: 24.4 us
  Pallas kernels  23.6 us (96%)
  local copies, waits for them, and re-layouts  0.73 us (3%)
    pallas_call x1, Pallas kernels, body(): pl.pallas_call(kernel, out_shape=pltpu.VMEM(state.shape, f32), in_specs=[...  23.6 us
    unnamed x1, local copies, waits for them, and re-layouts  0.73 us

profile of v8, /device:TPU:3, one launch (start us, length us, event | category | flops | bytes accessed | tf_op | source)
XLA Modules:
  0.0 24.4 jit_solution(5137527269576170060)
XLA Ops:
  0.0 23.6 %shard_map.55 = f32[1,20,2,16,128]{4,3,2,1,0:T(8,128)S(1)} custom-call(f32[1,20,2,16,128]{4,3,2,1,0:T(8,128)} %state_hbm.1, s32[4,2,16]{2,1,0:T(2,128)} %levels_hbm.1, f32[2,2,16,128]{3,2,1,0:T(8,128)} %flux_hbm.1, s32[19]{0:T(128)} %prey_hbm.1, f32[19]{0:T(128)} %rate_hbm.1), custom_call_target="tpu_custom_call" | custom-call | tf_op jit(solution)/shard_map/pallas_call | solution.py:371
  23.6 0.7 %copy.7 = f32[1,20,2,16,128]{4,3,2,1,0:T(8,128)} copy(f32[1,20,2,16,128]{4,3,2,1,0:T(8,128)S(1)} %shard_map.55) | data formatting | bytes 655360

commit v9 on v7

--- a/solution.py
+++ b/solution.py
@@ -20,8 +20,8 @@
 
 def kernel(
     state_hbm, levels_hbm, flux_hbm, prey_hbm, rate_hbm, out_ref,
-    levels_ref, prey_ref, rate_ref, raw, cur, tanhs, hx, ys, yr, wet, flux, run, light, heat,
-    load_sem, small_sem, send_sem, recv_sem, pair_send, pair_recv, ready_sem,
+    levels_ref, levels_by, halo_wet, prey_ref, rate_ref, raw, cur, tanhs, hx, ys, yr, wet, flux, run, light, heat,
+    load_sem, small_sem, send_sem, recv_sem, pair_send, pair_recv, ready_sem, by_send, by_recv,
 ):
     groups = cur.shape[1]
     size_x, size_y, depth = cur.shape[3:]
@@ -76,30 +76,63 @@
     diagonal = lax.broadcasted_iota(jnp.int32, (size_y, size_y), 0) == lax.broadcasted_iota(
         jnp.int32, (size_y, size_y), 1
     )
-    levels_load.wait()
-    for i in range(size_x):
+    run[...] = jnp.zeros(run.shape, jnp.float32)
+    heat[...] = jnp.zeros(heat.shape, jnp.float32)
+
+    def masks_of(line_of):
         active = []
         for c in range(4):
-            line = levels_ref[c, pl.ds(i, 1), :].astype(jnp.float32)
+            line = line_of(c).astype(jnp.float32)
             spread = jnp.where(diagonal, jnp.broadcast_to(line, (size_y, size_y)), 0.0)
             active.append(jnp.sum(spread, axis=1, keepdims=True))
         most = jnp.maximum(jnp.maximum(active[0], active[1]), jnp.maximum(active[2], active[3]))
-        for c in range(4):
-            mine = jnp.where(is_ocean, active[c], most)
-            wet[c, i] = jnp.where(level_k < mine, 1.0, 0.0)
-
-    run[...] = jnp.zeros(run.shape, jnp.float32)
-    heat[...] = jnp.zeros(heat.shape, jnp.float32)
-
-    def copy_of(s, g, side, ocean):
+        mine = [jnp.where(is_ocean, own, most) for own in active]
+        return [jnp.where(level_k < own, 1.0, 0.0) for own in mine]
+
+    def levels_copy(side):
+        return pltpu.make_async_remote_copy(
+            levels_hbm, levels_by.at[1 - side], by_send.at[side], by_recv.at[1 - side],
+            device_id=peer[side], device_id_type=MESH,
+        )
+
+    def own_masks():
+        levels_load.wait()
+        for i in range(size_x):
+            for c, mask in enumerate(masks_of(lambda c: levels_ref[c, pl.ds(i, 1), :])):
+                wet[c, i] = mask
+
+    def halo_masks():
+        for side in (WEST, EAST):
+            halo_wet[1, side] = jnp.ones(halo_wet.shape[2:], jnp.float32)
+
+            @pl.when(has[side])
+            def _():
+                pltpu.make_async_remote_copy(
+                    levels_by.at[side], levels_by.at[side], by_send.at[side], by_recv.at[side],
+                    device_id=peer[side], device_id_type=MESH,
+                ).wait_recv()
+                row = last_x if side == WEST else 0
+                masks = masks_of(lambda c: levels_by[side, c, pl.ds(row, 1), :])
+                for c in range(4):
+                    halo_wet[0, side, c] = masks[(c + 2) % 4 if side == WEST else c]
+
+            @pl.when(jnp.logical_not(has[side]))
+            def _():
+                halo_wet[0, side] = jnp.zeros(halo_wet.shape[2:], jnp.float32)
+
+    def copy_of(s, g, side, ocean, first=False):
         if side < 2:
             row = 0 if side == WEST else last_x
             if ocean:
                 channels = pl.ds(0, 2) if side == WEST else pl.ds(2, 2)
                 src = cur.at[s, g, channels, row]
+                if first:
+                    src = state_hbm.at[0, pl.ds(4 * g + (0 if side == WEST else 2), 2), row]
                 dst = hx.at[s, 1 - side, g, pl.ds(0, 2)]
             else:
                 src = cur.at[s, g, :, row]
+                if first:
+                    src = state_hbm.at[0, pl.ds(4 * g, 4), row]
                 dst = hx.at[s, 1 - side, g]
         else:
             src = ys.at[s, side - 2, g]
@@ -110,13 +143,33 @@
             device_id=peer[side], device_id_type=MESH,
         )
 
+    def start_y(s, g):
+        for side in (SOUTH, NORTH):
+            @pl.when(has[side])
+            def _():
+                copy_of(s, g, side, False).start()
+
+    def start_x(s, g, ocean, first=False):
+        for side, turn in ((WEST, even), (EAST, None), (WEST, jnp.logical_not(even))):
+            @pl.when(has[side] if turn is None else jnp.logical_and(has[side], turn))
+            def _():
+                copy_of(s, g, side, ocean, first).start()
+
     def start_copies(s, g, ocean):
-        for side, turn in (
-            (SOUTH, None), (NORTH, None), (WEST, even), (EAST, None), (WEST, jnp.logical_not(even)),
-        ):
-            @pl.when(has[side] if turn is None else jnp.logical_and(has[side], turn))
-            def _():
-                copy_of(s, g, side, ocean).start()
+        start_y(s, g)
+        start_x(s, g, ocean)
+
+    def start_first(ocean):
+        for side in (WEST, EAST):
+            @pl.when(has[side])
+            def _():
+                levels_copy(side).start()
+
+        def group(g, carry):
+            start_x(0, g, ocean, True)
+            return carry
+
+        lax.fori_loop(0, groups, group, 0)
 
     def wait_arrivals(s, g, ocean):
         for side in range(4):
@@ -136,6 +189,7 @@
             @pl.when(has[side])
             def _():
                 if side < 2:
+                    levels_copy(side).wait_send()
                     sent = hx.at[:, side, :, pl.ds(0, 2)] if ocean else hx.at[:, side]
                 else:
                     sent = yr.at[:, side - 2]
@@ -160,17 +214,24 @@
         arrived = yr[s, 0, g, pl.ds(c * size_x + i, 1), :]
         return jnp.where(rows == 0, arrived, pltpu.roll(value, 1, 0))
 
+    def beyond(s, side, g, c):
+        return hx[s, side, g, c] * halo_wet[jnp.minimum(s, 1), side, c]
+
     def ocean_part():
+        start_first(True)
+        own_masks()
+
         def first(g, carry):
             load(g).wait()
             put(0, g, [raw[g, c, i] * wet[c, i] for c, i in tiles])
-            start_copies(0, g, True)
+            start_y(0, g)
             return carry
 
         lax.fori_loop(0, groups, first, 0)
         flux_load.wait()
         prey_load.wait()
         rate_load.wait()
+        halo_masks()
 
         def pair_copy():
             return pltpu.make_async_remote_copy(
@@ -198,10 +259,10 @@
                     centre = cur[s, f, c, i]
                     if a == 0:
                         to_east = cur[s, f, 2 + b, i]
-                        to_west = cur[s, f, 2 + b, i - 1] if i > 0 else hx[s, WEST, f, b]
+                        to_west = cur[s, f, 2 + b, i - 1] if i > 0 else beyond(s, WEST, f, b)
                     else:
                         to_west = cur[s, f, b, i]
-                        to_east = cur[s, f, b, i + 1] if i < last_x else hx[s, EAST, f, b]
+                        to_east = cur[s, f, b, i + 1] if i < last_x else beyond(s, EAST, f, b)
                     other = cur[s, f, 2 * a + 1 - b, i]
                     if b == 0:
                         to_north = other
@@ -241,11 +302,14 @@
         pair_copy().wait_send()
 
     def tracer_part():
+        start_first(False)
+        own_masks()
+
         def first(g, carry):
             load(g).wait()
             values = [raw[g, c, i] * wet[c, i] for c, i in tiles]
             put(0, g, values)
-            start_copies(0, g, False)
+            start_y(0, g)
             for (c, i), value in zip(tiles, values):
                 tanhs[0, 4 * g + c, i] = jnp.tanh(value)
             return carry
@@ -254,6 +318,7 @@
         flux_load.wait()
         prey_load.wait()
         rate_load.wait()
+        halo_masks()
 
         def pair_copy():
             return pltpu.make_async_remote_copy(
@@ -283,8 +348,8 @@
                     prey = prey_ref[slot]
                     for i in range(size_x):
                         centre = cur[s, g, c, i]
-                        to_west = cur[s, g, c, i - 1] if i > 0 else hx[s, WEST, g, c]
-                        to_east = cur[s, g, c, i + 1] if i < last_x else hx[s, EAST, g, c]
+                        to_west = cur[s, g, c, i - 1] if i > 0 else beyond(s, WEST, g, c)
+                        to_east = cur[s, g, c, i + 1] if i < last_x else beyond(s, EAST, g, c)
                         to_north = north_of(centre, s, g, c, i)
                         to_south = south_of(centre, s, g, c, i)
                         spread = to_east + to_west + to_north + to_south - 4.0 * centre
@@ -355,6 +420,8 @@
         out_specs=pl.BlockSpec(memory_space=pltpu.VMEM),
         scratch_shapes=[
             pltpu.VMEM(levels.shape, levels.dtype),
+            pltpu.VMEM((2,) + levels.shape, levels.dtype),
+            pltpu.VMEM((2, 2, 4, size_y, depth), f32),
             pltpu.SMEM(eco_prey.shape, eco_prey.dtype),
             pltpu.SMEM(eco_rate.shape, eco_rate.dtype),
             pltpu.VMEM((groups, 4) + tile, f32),
@@ -375,6 +442,8 @@
             pltpu.SemaphoreType.DMA,
             pltpu.SemaphoreType.DMA,
             pltpu.SemaphoreType.REGULAR,
+            pltpu.SemaphoreType.DMA((2,)),
+            pltpu.SemaphoreType.DMA((2,)),
         ],
         compiler_params=pltpu.CompilerParams(
             collective_id=0, has_side_effects=True, vmem_limit_bytes=60 * 1024 * 1024

time: 24.4 us -> 24.7 us (1.012)
  Pallas kernels: 23.5 us -> 23.8 us
    pallas_call x1, Pallas kernels: 23.5 us -> 23.8 us  [body(): pl.pallas_call(kernel, out_shape=pltpu.VMEM(state.shape, f32), in_specs=[...]
where the time goes in v9:
time: 24.7 us; the launch traced here: 24.5 us
  Pallas kernels  23.8 us (96%)
  local copies, waits for them, and re-layouts  0.73 us (3%)
    pallas_call x1, Pallas kernels, body(): pl.pallas_call(kernel, out_shape=pltpu.VMEM(state.shape, f32), in_specs=[...  23.8 us
    unnamed x1, local copies, waits for them, and re-layouts  0.73 us

profile of v9, /device:TPU:3, one launch (start us, length us, event | category | flops | bytes accessed | tf_op | source)
XLA Modules:
  0.0 24.5 jit_solution(4281941069755983553)
XLA Ops:
  0.0 23.8 %shard_map.55 = f32[1,20,2,16,128]{4,3,2,1,0:T(8,128)S(1)} custom-call(f32[1,20,2,16,128]{4,3,2,1,0:T(8,128)} %state_hbm.1, s32[4,2,16]{2,1,0:T(2,128)} %levels_hbm.1, f32[2,2,16,128]{3,2,1,0:T(8,128)} %flux_hbm.1, s32[19]{0:T(128)} %prey_hbm.1, f32[19]{0:T(128)} %rate_hbm.1), custom_call_target="tpu_custom_call" | custom-call | tf_op jit(solution)/shard_map/pallas_call | solution.py:416
  23.8 0.7 %copy.7 = f32[1,20,2,16,128]{4,3,2,1,0:T(8,128)} copy(f32[1,20,2,16,128]{4,3,2,1,0:T(8,128)S(1)} %shard_map.55) | data formatting | bytes 655360

commit v10 on v9

--- a/solution.py
+++ b/solution.py
@@ -14,6 +14,7 @@
 MORTALITY = 0.1
 HEATING = 2.0
 SURFACE = 8.0
+AHEAD = 2
 MESH = pl.DeviceIdType.MESH
 WEST, EAST, SOUTH, NORTH = 0, 1, 2, 3
 
@@ -169,7 +170,7 @@
             start_x(0, g, ocean, True)
             return carry
 
-        lax.fori_loop(0, groups, group, 0)
+        lax.fori_loop(0, AHEAD, group, 0)
 
     def wait_arrivals(s, g, ocean):
         for side in range(4):
@@ -225,6 +226,11 @@
             load(g).wait()
             put(0, g, [raw[g, c, i] * wet[c, i] for c, i in tiles])
             start_y(0, g)
+
+            @pl.when(g >= AHEAD)
+            def _():
+                start_x(0, g, True, True)
+
             return carry
 
         lax.fori_loop(0, groups, first, 0)
@@ -310,6 +316,11 @@
             values = [raw[g, c, i] * wet[c, i] for c, i in tiles]
             put(0, g, values)
             start_y(0, g)
+
+            @pl.when(g >= AHEAD)
+            def _():
+                start_x(0, g, False, True)
+
             for (c, i), value in zip(tiles, values):
                 tanhs[0, 4 * g + c, i] = jnp.tanh(value)
             return carry

time: 24.7 us -> 24.7 us (level)
  no operation moved by 1% of the time
where the time goes in v10:
time: 24.7 us; the launch traced here: 24.5 us
  Pallas kernels  23.8 us (96%)
  local copies, waits for them, and re-layouts  0.73 us (3%)
    pallas_call x1, Pallas kernels, body(): pl.pallas_call(kernel, out_shape=pltpu.VMEM(state.shape, f32), in_specs=[...  23.8 us
    unnamed x1, local copies, waits for them, and re-layouts  0.73 us

profile of v10, /device:TPU:3, one launch (start us, length us, event | category | flops | bytes accessed | tf_op | source)
XLA Modules:
  0.0 24.5 jit_solution(5570619916242080306)
XLA Ops:
  0.0 23.8 %shard_map.55 = f32[1,20,2,16,128]{4,3,2,1,0:T(8,128)S(1)} custom-call(f32[1,20,2,16,128]{4,3,2,1,0:T(8,128)} %state_hbm.1, s32[4,2,16]{2,1,0:T(2,128)} %levels_hbm.1, f32[2,2,16,128]{3,2,1,0:T(8,128)} %flux_hbm.1, s32[19]{0:T(128)} %prey_hbm.1, f32[19]{0:T(128)} %rate_hbm.1), custom_call_target="tpu_custom_call" | custom-call | tf_op jit(solution)/shard_map/pallas_call | solution.py:427
  23.8 0.7 %copy.7 = f32[1,20,2,16,128]{4,3,2,1,0:T(8,128)} copy(f32[1,20,2,16,128]{4,3,2,1,0:T(8,128)S(1)} %shard_map.55) | data formatting | bytes 655360

commit v11 on v7

--- a/solution.py
+++ b/solution.py
@@ -35,6 +35,7 @@
     peer = ((half, gx - 1, gy), (half, gx + 1, gy), (half, gx, gy - 1), (half, gx, gy + 1))
     partner = (1 - half, gx, gy)
     even = lax.rem(gy, 2) == 0
+    batches = ((0, groups // 2), (groups // 2, groups - groups // 2))
 
     def load(g):
         return pltpu.make_async_copy(state_hbm.at[0, pl.ds(4 * g, 4)], raw.at[g], load_sem.at[g])
@@ -92,44 +93,56 @@
     heat[...] = jnp.zeros(heat.shape, jnp.float32)
 
     def copy_of(s, g, side, ocean):
-        if side < 2:
-            row = 0 if side == WEST else last_x
-            if ocean:
-                channels = pl.ds(0, 2) if side == WEST else pl.ds(2, 2)
-                src = cur.at[s, g, channels, row]
-                dst = hx.at[s, 1 - side, g, pl.ds(0, 2)]
-            else:
-                src = cur.at[s, g, :, row]
-                dst = hx.at[s, 1 - side, g]
+        row = 0 if side == WEST else last_x
+        if ocean:
+            channels = pl.ds(0, 2) if side == WEST else pl.ds(2, 2)
+            src = cur.at[s, g, channels, row]
+            dst = hx.at[s, 1 - side, g, pl.ds(0, 2)]
         else:
-            src = ys.at[s, side - 2, g]
-            dst = yr.at[s, 3 - side, g]
-        lands = 1 - side if side < 2 else 5 - side
+            src = cur.at[s, g, :, row]
+            dst = hx.at[s, 1 - side, g]
         return pltpu.make_async_remote_copy(
-            src, dst, send_sem.at[side], recv_sem.at[s, g, lands],
+            src, dst, send_sem.at[side], recv_sem.at[s, g, 1 - side],
             device_id=peer[side], device_id_type=MESH,
         )
 
+    def y_copy(s, n, side):
+        span = pl.ds(*batches[n])
+        return pltpu.make_async_remote_copy(
+            ys.at[s, side - 2, span], yr.at[s, 3 - side, span],
+            send_sem.at[side], recv_sem.at[s, n, 5 - side],
+            device_id=peer[side], device_id_type=MESH,
+        )
+
     def start_copies(s, g, ocean):
-        for side, turn in (
-            (SOUTH, None), (NORTH, None), (WEST, even), (EAST, None), (WEST, jnp.logical_not(even)),
-        ):
+        for n, (low, count) in enumerate(batches):
+            for side in (SOUTH, NORTH):
+                @pl.when(jnp.logical_and(g == low + count - 1, has[side]))
+                def _():
+                    y_copy(s, n, side).start()
+        for side, turn in ((WEST, even), (EAST, None), (WEST, jnp.logical_not(even))):
             @pl.when(has[side] if turn is None else jnp.logical_and(has[side], turn))
             def _():
                 copy_of(s, g, side, ocean).start()
 
+    def arrival(condition, lands, side, sem):
+        @pl.when(condition)
+        def _():
+            pltpu.make_async_remote_copy(
+                lands, lands, send_sem.at[side], sem,
+                device_id=peer[side], device_id_type=MESH,
+            ).wait_recv()
+
     def wait_arrivals(s, g, ocean):
-        for side in range(4):
-            @pl.when(has[side])
-            def _():
-                if side < 2:
-                    lands = hx.at[s, side, g, pl.ds(0, 2)] if ocean else hx.at[s, side, g]
-                else:
-                    lands = yr.at[s, side - 2, g]
-                pltpu.make_async_remote_copy(
-                    lands, lands, send_sem.at[side], recv_sem.at[s, g, side],
-                    device_id=peer[side], device_id_type=MESH,
-                ).wait_recv()
+        for n, (low, count) in enumerate(batches):
+            for side in (SOUTH, NORTH):
+                arrival(
+                    jnp.logical_and(g == low, has[side]),
+                    yr.at[s, side - 2, pl.ds(low, count)], side, recv_sem.at[s, n, side],
+                )
+        for side in (WEST, EAST):
+            lands = hx.at[s, side, g, pl.ds(0, 2)] if ocean else hx.at[s, side, g]
+            arrival(has[side], lands, side, recv_sem.at[s, g, side])
 
     def wait_sends(ocean):
         for side in range(4):

time: 24.4 us -> 24.7 us (1.012)
  Pallas kernels: 23.5 us -> 23.8 us
    pallas_call x1, Pallas kernels: 23.5 us -> 23.8 us  [body(): pl.pallas_call(kernel, out_shape=pltpu.VMEM(state.shape, f32), in_specs=[...]
where the time goes in v11:
time: 24.7 us; the launch traced here: 24.6 us
  Pallas kernels  23.8 us (96%)
  local copies, waits for them, and re-layouts  0.73 us (3%)
    pallas_call x1, Pallas kernels, body(): pl.pallas_call(kernel, out_shape=pltpu.VMEM(state.shape, f32), in_specs=[...  23.8 us
    unnamed x1, local copies, waits for them, and re-layouts  0.73 us

profile of v11, /device:TPU:3, one launch (start us, length us, event | category | flops | bytes accessed | tf_op | source)
XLA Modules:
  0.0 24.6 jit_solution(434671402701493141)
XLA Ops:
  0.0 23.8 %shard_map.55 = f32[1,20,2,16,128]{4,3,2,1,0:T(8,128)S(1)} custom-call(f32[1,20,2,16,128]{4,3,2,1,0:T(8,128)} %state_hbm.1, s32[4,2,16]{2,1,0:T(2,128)} %levels_hbm.1, f32[2,2,16,128]{3,2,1,0:T(8,128)} %flux_hbm.1, s32[19]{0:T(128)} %prey_hbm.1, f32[19]{0:T(128)} %rate_hbm.1), custom_call_target="tpu_custom_call" | custom-call | tf_op jit(solution)/shard_map/pallas_call | solution.py:364
  23.8 0.7 %copy.7 = f32[1,20,2,16,128]{4,3,2,1,0:T(8,128)} copy(f32[1,20,2,16,128]{4,3,2,1,0:T(8,128)S(1)} %shard_map.55) | data formatting | bytes 655360

commit v12 on v7

--- a/solution.py
+++ b/solution.py
@@ -306,7 +306,7 @@
                     out_ref[0, 4 * g + c, i] = value
                     tanhs[later, 4 * g + c, i] = jnp.tanh(value)
 
-                @pl.when(jnp.logical_and(s == NSUB - 1, g == 0))
+                @pl.when(jnp.logical_and(s == NSUB - 1, g == groups // 2))
                 def _():
                     above = (
                         lax.broadcasted_iota(jnp.int32, (depth, depth), 0)

time: 24.4 us -> 24.7 us (1.012); the launches traced: 24.2 us -> 24.2 us
  no operation moved by 1% of the time
where the time goes in v12:
time: 24.7 us; the launch traced here: 24.2 us
  Pallas kernels  23.5 us (95%)
  local copies, waits for them, and re-layouts  0.73 us (3%)
    pallas_call x1, Pallas kernels, body(): pl.pallas_call(kernel, out_shape=pltpu.VMEM(state.shape, f32), in_specs=[...  23.5 us
    unnamed x1, local copies, waits for them, and re-layouts  0.73 us

profile of v12, /device:TPU:3, one launch (start us, length us, event | category | flops | bytes accessed | tf_op | source)
XLA Modules:
  0.0 24.2 jit_solution(5292084212965831739)
XLA Ops:
  0.0 23.5 %shard_map.55 = f32[1,20,2,16,128]{4,3,2,1,0:T(8,128)S(1)} custom-call(f32[1,20,2,16,128]{4,3,2,1,0:T(8,128)} %state_hbm.1, s32[4,2,16]{2,1,0:T(2,128)} %levels_hbm.1, f32[2,2,16,128]{3,2,1,0:T(8,128)} %flux_hbm.1, s32[19]{0:T(128)} %prey_hbm.1, f32[19]{0:T(128)} %rate_hbm.1), custom_call_target="tpu_custom_call" | custom-call | tf_op jit(solution)/shard_map/pallas_call | solution.py:351
  23.5 0.7 %copy.7 = f32[1,20,2,16,128]{4,3,2,1,0:T(8,128)} copy(f32[1,20,2,16,128]{4,3,2,1,0:T(8,128)S(1)} %shard_map.55) | data formatting | bytes 655360
